TPU v7x, 32 devices: a whole 2x2x4 slice. The times are simulated.
32 devices in a mesh: expert: 8 (over z, x), tensor: 4 (over y, core).
Axes of the slice: x: 2, y: 2, z: 4, core: 2. Of those that a mesh axis runs over, the one named last changes fastest.
Arguments:
- inputs: bfloat16 [16384, 768], P(('expert', 'tensor')), may hold values from -6 to 6
- lengths: int32 [16], P('expert'), may hold values from 512 to 1024, as said below
- routes: int32 [16384, 2], P(('expert', 'tensor')), may hold values from 0 to 7, all different within a row; in each aligned block of 512 rows (0 to 511, 512 to 1023, ...) at most 256 rows name the same one
- attn_gain: float32 [768], replicated, may hold values from 0.25 to 1.75
- qkv_weight: bfloat16 [768, 3, 768], P(None, None, 'tensor'), may hold values from -0.21875 to 0.21875
- out_weight: bfloat16 [768, 768], P('tensor'), may hold values from -1.5 to 1.5
- rel_bias: float32 [32, 12], P(None, 'tensor'), may hold values from -4 to 4
- moe_gain: float32 [768], replicated, may hold values from 0.25 to 1.75
- router_weight: bfloat16 [768, 8], replicated, may hold values from -0.15625 to 0.15625
- up_weight: bfloat16 [8, 768, 3072], P('expert', None, 'tensor'), may hold values from -0.21875 to 0.21875
- down_weight: bfloat16 [8, 3072, 768], P('expert', 'tensor'), may hold values from -0.109375 to 0.109375
- out_grad: bfloat16 [16384, 768], P(('expert', 'tensor')), may hold values from -6 to 6
Outputs:
- outputs: bfloat16 [16384, 768], P(('expert', 'tensor'))
- grad_inputs: bfloat16 [16384, 768], P(('expert', 'tensor'))
- grad_attn_gain: float32 [768], replicated
- grad_qkv_weight: float32 [768, 3, 768], P(None, None, 'tensor')
- grad_out_weight: float32 [768, 768], P('tensor')
- grad_rel_bias: float32 [32, 12], P(None, 'tensor')
- grad_moe_gain: float32 [768], replicated
- grad_router: float32 [768, 8], replicated
- grad_up: float32 [8, 768, 3072], P('expert', None, 'tensor')
- grad_down: float32 [8, 3072, 768], P('expert', 'tensor')
Inputs may be any that keep to these rules, and one draw needn't show every extreme that they name: `lengths`: each sequence's real tokens come first, the rest of its 1024 slots are padding; some sequence fills all 1024 slots. `routes`: A token names two different experts. Among the rows of one device no expert is named more than 256 times, and in every draw some device names some expert exactly 256 times.
All inputs are finite; a program needn't handle non-finite values.
Results may differ from a plain program's by a relative error of at most 0.017.
Values may be sent and summed in bfloat16 or wider, within the bound.
A program may use at most 192 MiB of HBM per device.

v0:
```python
import functools

import jax
import jax.numpy as jnp
from jax import lax
from jax.experimental import pallas as pl
from jax.experimental.pallas import tpu as pltpu
from jax.sharding import PartitionSpec as P

D = 768
HD = 64
NB = 32
MAXDIST = 128
SEQ = 1024
EPSILON = 1e-06
NEGATIVE = -1e30
TILE = 256
BF = jnp.bfloat16
F32 = jnp.float32
MIB = 2**20
CHUNK = 256
GELU = 0.7978845608028654
CUBIC = 0.044715


def bucket_edges():
    half_count = NB // 2
    short_edges = list(range(1, half_count))
    long_edges = [
        int(half_count * (MAXDIST / half_count) ** (step_index / half_count))
        for step_index in range(half_count)
    ]
    return short_edges + long_edges


EDGES = bucket_edges()


def dot(a, b, ca=1, cb=0, precision=None):
    return lax.dot_general(
        a, b, (((ca,), (cb,)), ((), ())), preferred_element_type=F32, precision=precision
    )


def iota(shape, dim):
    return lax.broadcasted_iota(jnp.int32, shape, dim)


def rms(v):
    return lax.rsqrt(jnp.mean(v * v, axis=-1, keepdims=True) + EPSILON)


def call(kernel, outs, args, specs=None, scratch=(), flops=0, moved=0, exps=0, vmem=56, name=None):
    vm = pl.BlockSpec(memory_space=pltpu.VMEM)
    return pl.pallas_call(
        kernel,
        out_shape=[jax.ShapeDtypeStruct(s, d) for s, d in outs],
        in_specs=specs or [vm] * len(args),
        out_specs=[vm] * len(outs),
        scratch_shapes=list(scratch),
        compiler_params=pltpu.CompilerParams(vmem_limit_bytes=vmem * MIB),
        cost_estimate=pl.CostEstimate(flops=flops, bytes_accessed=moved, transcendentals=exps),
        name=name,
    )(*args)


def own_length(lengths_ref):
    return lengths_ref[lax.axis_index("tensor") // 2]


def own_valid(lengths_ref, rows):
    half = lax.rem(lax.axis_index("tensor"), 2)
    return jnp.clip(own_length(lengths_ref) - half * rows, 0, rows)


VM = pl.BlockSpec(memory_space=pltpu.VMEM)
SM = pl.BlockSpec(memory_space=pltpu.SMEM)


def slot_lines(experts, cap, valid_count, routes):
    rows = routes.shape[1]
    valid = iota((1, rows), 1) < valid_count
    ids = iota((experts, rows), 0)
    hot0 = ((ids == routes[0:1]) & valid).astype(F32)
    hot1 = ((ids == routes[1:2]) & valid).astype(F32)
    before = (iota((rows, rows), 0) < iota((rows, rows), 1)).astype(BF)
    rank = dot((hot0 + hot1).astype(BF), before)
    place = ids.astype(F32) * cap + rank
    bad = jnp.where(valid, 0.0, 1.0)
    slot0 = jnp.sum(hot0 * place, axis=0, keepdims=True) - bad
    slot1 = jnp.sum(hot1 * place, axis=0, keepdims=True) - bad
    return slot0, slot1


def route_kernel(experts, cap, lengths_ref, routes_ref, grad_ref, packed_ref, slots_ref):
    rows = grad_ref.shape[0]
    slot0, slot1 = slot_lines(experts, cap, own_valid(lengths_ref, routes_ref.shape[1]), routes_ref[...])
    spots = iota((experts * cap, rows), 0)
    pick0 = spots == slot0.astype(jnp.int32)
    pick1 = spots == slot1.astype(jnp.int32)
    packed_ref[...] = dot((pick0 | pick1).astype(BF), grad_ref[...]).astype(BF)
    slots_ref[...] = jnp.concatenate([slot0, slot1, jnp.zeros((6, rows), F32)], axis=0)


def slots_kernel(experts, cap, lengths_ref, routes_ref, slots_ref):
    rows = routes_ref.shape[1]
    slot0, slot1 = slot_lines(experts, cap, own_valid(lengths_ref, routes_ref.shape[1]), routes_ref[...])
    slots_ref[...] = jnp.concatenate([slot0, slot1, jnp.zeros((6, rows), F32)], axis=0)


def back_matrix(slots_ref, spots):
    rows = slots_ref.shape[1]
    where = iota((rows, spots), 1)
    slots = slots_ref[...].T.astype(jnp.int32)
    return ((where == slots[:, 0:1]) | (where == slots[:, 1:2])).astype(BF)


def bias_tiles(table_ref, head):
    dist = iota((8, TILE), 1)
    line = table_ref[head : head + 1, :]
    line = line - line[:, NB - 1 :]
    curve = jnp.broadcast_to(line[:, 0:1], (8, TILE))
    for number, edge in enumerate(EDGES):
        curve = jnp.where(dist >= edge, line[:, number + 1 : number + 2], curve)
    spread = jnp.broadcast_to(curve[0:1], (TILE, TILE))
    ring = pltpu.roll(spread, 0, 1, stride=1, stride_axis=0)
    ahead = iota((TILE, TILE), 1) >= iota((TILE, TILE), 0)
    return jnp.where(ahead, ring, NEGATIVE), jnp.where(ahead, 0.0, ring)


def head_pieces(qkvt_ref, mask_rows, head, local_inner):
    start = pl.multiple_of(head * HD, HD)
    q = qkvt_ref[pl.ds(start, HD), :] * jnp.asarray(HD**-0.5, BF)
    k = qkvt_ref[pl.ds(local_inner + start, HD), :]
    v = qkvt_ref[pl.ds(2 * local_inner + start, HD), :]
    ones = jnp.ones((16, SEQ), BF)
    return jnp.concatenate([q, ones], 0), jnp.concatenate([k, mask_rows], 0), v, ones


def mask_block(length):
    keep = (iota((16, SEQ), 1) < length) | (iota((16, SEQ), 0) > 0)
    return jnp.where(keep, 0.0, NEGATIVE).astype(BF)


def score_pieces(k, q, block, near, below):
    cols = slice(block * TILE, (block + 1) * TILE)
    qb = q[:, cols]
    pieces = []
    if block >= 2:
        pieces.append((0, (block - 1) * TILE, dot(k[: (block - 1) * TILE], qb)))
    if block >= 1:
        lo = (block - 1) * TILE
        pieces.append((lo, block * TILE, dot(k[lo : lo + TILE], qb) + below))
    lo = block * TILE
    pieces.append((lo, lo + TILE, dot(k[lo : lo + TILE], qb) + near))
    return cols, pieces


def attn_fwd_kernel(first, heads, lengths_ref, table_ref, *refs):
    if first:
        own_ref, other_ref, gain_ref, w_ref, ow_ref = refs[:5]
        normed_ref, qkvt_ref, mixt_ref, lse_ref, part_ref = refs[5:]
        half = own_ref.shape[0]
        core = lax.rem(lax.axis_index("tensor"), 2)
        for source, place in ((own_ref, core), (other_ref, 1 - core)):
            x = source[...].astype(F32)
            normed_ref[pl.ds(pl.multiple_of(place * half, half), half), :] = (
                x * rms(x) * gain_ref[...]
            ).astype(BF)
    else:
        normed_ref, w_ref, ow_ref, part_in = refs[:4]
        qkvt_ref, mixt_ref, lse_ref, keep_ref, send_ref, part_ref = refs[4:]
    local_inner = heads * HD
    qkvt_ref[...] = dot(w_ref[...], normed_ref[...], 1, 1).astype(BF)
    masks = mask_block(own_length(lengths_ref))
    lse_ref[...] = jnp.zeros_like(lse_ref)

    for head in range(heads):
        near, below = bias_tiles(table_ref, head)
        q, kt, v, ones = head_pieces(qkvt_ref, masks, head, local_inner)
        k = kt.T
        vx = jnp.concatenate([v, ones], 0)
        for block in range(SEQ // TILE):
            cols, pieces = score_pieces(k, q, block, near, below)
            top = functools.reduce(
                jnp.maximum, [jnp.max(s, axis=0, keepdims=True) for _, _, s in pieces]
            )
            total = None
            for lo, hi, s in pieces:
                term = dot(vx[:, lo:hi], jnp.exp(s - top).astype(BF))
                total = term if total is None else total + term
            weight = total[HD : HD + 1]
            mixt_ref[head * HD : (head + 1) * HD, cols] = (total[:HD] / weight).astype(BF)
            lse_ref[head : head + 1, cols] = top + jnp.log(weight)
    part = dot(mixt_ref[...], ow_ref[...], 0, 0)
    if first:
        part_ref[...] = part
    else:
        part_ref[...] = part + part_in[...]
        half = keep_ref.shape[0]
        core = lax.rem(lax.axis_index("tensor"), 2)
        keep_ref[...] = part_ref[pl.ds(pl.multiple_of(core * half, half), half), :]
        send_ref[...] = part_ref[pl.ds(pl.multiple_of((1 - core) * half, half), half), :].astype(BF)


def attn_bwd_kernel(last, heads, lengths_ref, table_ref, *refs):
    if last:
        (normed_ref, w_ref, ow_ref, qkvt_ref, mixt_ref, lse_ref, own_ref, other_ref, part_in) = refs[:9]
        gw_ref, gbias_ref, keep_ref, send_ref, ga_ref, got_ref, gt_ref, d0_ref, d1_ref, part_ref = refs[9:]
    else:
        (normed_ref, w_ref, ow_ref, qkvt_ref, mixt_ref, lse_ref, own_ref, other_ref) = refs[:8]
        gw_ref, gbias_ref, part_ref, ga_ref, got_ref, gt_ref, d0_ref, d1_ref = refs[8:]
    local_inner = heads * HD
    half = own_ref.shape[0]
    core = lax.rem(lax.axis_index("tensor"), 2)
    ga_ref[pl.ds(pl.multiple_of(core * half, half), half), :] = own_ref[...]
    ga_ref[pl.ds(pl.multiple_of((1 - core) * half, half), half), :] = other_ref[...]
    got_ref[...] = dot(ow_ref[...], ga_ref[...], 1, 1).astype(BF)
    gw_ref[3 * local_inner :] = dot(mixt_ref[...], ga_ref[...]).astype(gw_ref.dtype)
    masks = mask_block(own_length(lengths_ref))
    gbias_ref[...] = jnp.zeros_like(gbias_ref)
    ahead = iota((TILE, TILE), 1) >= iota((TILE, TILE), 0)
    spot = (iota((TILE, 128), 0) + 1) % TILE
    flip = (iota((TILE, TILE), 0) + iota((TILE, TILE), 1) == TILE - 1).astype(F32)
    bucket = jnp.zeros((TILE, 128), jnp.int32)
    for edge in EDGES:
        bucket = bucket + (spot >= edge).astype(jnp.int32)
    hot = (bucket == iota((TILE, 128), 1)).astype(F32)

    for head in range(heads):
        near, below = bias_tiles(table_ref, head)
        q, kt, vt, _ = head_pieces(qkvt_ref, masks, head, local_inner)
        k = kt.T
        v = vt.T
        rows = slice(head * HD, (head + 1) * HD)
        gt = got_ref[rows, :]
        delta = jnp.sum(gt.astype(F32) * mixt_ref[rows, :].astype(F32), axis=0, keepdims=True)
        gk = [None] * (SEQ // TILE)
        gv = [None] * (SEQ // TILE)
        far = jnp.zeros((8, TILE), F32)
        for block in range(SEQ // TILE):
            cols, pieces = score_pieces(k, q, block, near, below)
            gb = gt[:, cols]
            qb = q[:HD, cols]
            lse = lse_ref[head : head + 1, cols]
            db = delta[:, cols]
            gq = None
            for lo, hi, s in pieces:
                p = jnp.exp(s - lse)
                ds = p * (dot(v[lo:hi], gb) - db)
                pb = p.astype(BF)
                dsb = ds.astype(BF)
                term = dot(kt[:HD, lo:hi], dsb)
                gq = term if gq is None else gq + term
                tv = dot(pb, gb, 1, 1)
                tk = dot(dsb, qb, 1, 1)
                for tile in range(lo // TILE, hi // TILE):
                    part = slice(tile * TILE - lo, (tile + 1) * TILE - lo)
                    gv[tile] = tv[part] if gv[tile] is None else gv[tile] + tv[part]
                    gk[tile] = tk[part] if gk[tile] is None else gk[tile] + tk[part]
                if hi == (block + 1) * TILE:
                    d0_ref[...] = ds if block == 0 else d0_ref[...] + ds
                elif hi == block * TILE and lo == (block - 1) * TILE:
                    d1_ref[...] = ds if block == 1 else d1_ref[...] + ds
                else:
                    far = far + jnp.sum(ds.reshape((hi - lo) // 8, 8, TILE), axis=0)
            gt_ref[rows, cols] = (gq * HD**-0.5).astype(BF)
        for tile in range(SEQ // TILE):
            cols = slice(tile * TILE, (tile + 1) * TILE)
            gt_ref[local_inner + head * HD : local_inner + (head + 1) * HD, cols] = (
                gk[tile].T.astype(BF)
            )
            gt_ref[2 * local_inner + head * HD : 2 * local_inner + (head + 1) * HD, cols] = (
                gv[tile].T.astype(BF)
            )
        d1 = d1_ref[...]
        ring = jnp.where(ahead, d0_ref[...], d1)
        turned = pltpu.roll(
            dot(flip, ring, 1, 0, lax.Precision.HIGHEST), 0, 1, stride=1, stride_axis=0
        )
        far = far + jnp.sum(jnp.where(ahead, d1, 0.0).reshape(TILE // 8, 8, TILE), axis=0)
        line = jnp.sum(turned, axis=0, keepdims=True)
        sums = dot(
            jnp.broadcast_to(line, (8, TILE)), hot, 1, 0, lax.Precision.HIGHEST
        )
        sums = sums + jnp.where(iota((8, 128), 1) == NB - 1, jnp.sum(far), 0.0)
        gbias_ref[head : head + 1, :] = sums[0:1]
    gw_ref[: 3 * local_inner] = dot(gt_ref[...], normed_ref[...]).astype(gw_ref.dtype)
    part = dot(gt_ref[...], w_ref[...], 0, 0)
    if last:
        part_ref[...] = part + part_in[...]
        keep_ref[...] = part_ref[pl.ds(pl.multiple_of(core * half, half), half), :]
        send_ref[...] = part_ref[pl.ds(pl.multiple_of((1 - core) * half, half), half), :].astype(BF)
    else:
        part_ref[...] = part


def gates_of(experts, normed, router_t, routes):
    rows = normed.shape[0]
    logits = dot(router_t, normed, 1, 1)
    ids = iota((experts, rows), 0)
    signs = (ids == routes[0:1]).astype(F32) - (ids == routes[1:2]).astype(F32)
    gap = jnp.sum(logits * signs, axis=0, keepdims=True)
    return 1.0 / (1.0 + jnp.exp(-gap)), 1.0 / (1.0 + jnp.exp(gap))


def meta_lines(gate, code):
    rows = gate.shape[1]
    line = iota((8, rows), 0)
    high = gate.astype(BF).astype(F32)
    mid = (gate - high).astype(BF).astype(F32)
    low = gate - high - mid
    picked = jnp.where(line == 0, high, jnp.where(line == 1, mid, jnp.where(line == 2, low, 0.0)))
    return jnp.where(line == 3, code, picked).astype(BF)


def hidden_rows(x_ref, keep_ref, got_ref, gain_ref, hidden_ref):
    hidden = x_ref[...].astype(F32) + keep_ref[...] + got_ref[...].astype(F32)
    hidden_ref[...] = hidden
    return (hidden * rms(hidden) * gain_ref[...]).astype(BF)


def middle_kernel(
    experts, cap, x_ref, keep_ref, got_ref, gain_ref, router_ref, routes_ref, slots_ref, hidden_ref, packed_ref, meta_ref
):
    normed = hidden_rows(x_ref, keep_ref, got_ref, gain_ref, hidden_ref)
    slots = slots_ref[...].astype(jnp.int32)
    routes = routes_ref[...]
    where = iota((experts * cap, normed.shape[0]), 0)
    pick0 = where == slots[0:1]
    pick1 = where == slots[1:2]
    packed_ref[...] = dot((pick0 | pick1).astype(BF), normed).astype(BF)
    gate0, gate1 = gates_of(experts, normed, router_ref[...], routes)
    codes = (routes + 1).astype(F32)
    meta = dot(meta_lines(gate0, codes[1:2]), pick0.astype(BF), 1, 1) + dot(
        meta_lines(gate1, codes[0:1]), pick1.astype(BF), 1, 1
    )
    for number in range(experts):
        meta_ref[number] = meta[:, number * cap : (number + 1) * cap]


def middle_line_kernel(
    experts, x_ref, keep_ref, got_ref, gain_ref, router_ref, routes_ref, slots_ref, hidden_ref, normed_ref, info_ref
):
    normed = hidden_rows(x_ref, keep_ref, got_ref, gain_ref, hidden_ref)
    normed_ref[...] = normed
    routes = routes_ref[...]
    gate0, gate1 = gates_of(experts, normed, router_ref[...], routes)
    codes = (routes + 1).astype(F32)
    info_ref[...] = jnp.concatenate(
        [slots_ref[0:2], gate0, gate1, codes, jnp.zeros((2, normed.shape[0]), F32)], axis=0
    )


def gelu_pair(v):
    squared = v * v
    slope = GELU * (1.0 + 3 * CUBIC * squared)
    t = jnp.tanh(v * (GELU + GELU * CUBIC * squared))
    half = 0.5 + 0.5 * t
    return v * half, half + 0.5 * v * (1.0 - t * t) * slope


def flipped(me, k, count):
    total, bit = 0, 1
    while bit < count:
        total = total + lax.rem(me // bit + k // bit, 2) * bit
        bit *= 2
    return total


def weight_grads(xt_ref, geot_ref, act_ref, gi_ref, stage_ref, stay_ref, away_ref, go_ref, out_sem):
    tiles = D // TILE
    steps = 8 * tiles

    def columns(step):
        return pl.ds(pl.multiple_of(lax.rem(step, tiles) * TILE, TILE), TILE)

    def store(step, slot, out_ref):
        half = lax.rem(step, 2 * tiles) // tiles
        return pltpu.make_async_copy(
            stage_ref.at[slot],
            out_ref.at[pl.ds(pl.multiple_of(half * D, D), D), columns(step)],
            out_sem.at[slot],
        )

    def weights(step, carry):
        q = step // (2 * tiles)
        half = lax.rem(step, 2 * tiles) // tiles
        slot = lax.rem(step, 2)

        @pl.when(step >= 2)
        def _():
            store(step - 2, slot, stay_ref).wait()

        @pl.when(half == 0)
        def _():
            stage_ref[slot] = dot(xt_ref[...], gi_ref[q, :, columns(step)]).astype(BF)

        @pl.when(half == 1)
        def _():
            stage_ref[slot] = dot(geot_ref[...], act_ref[q, :, columns(step)]).astype(BF)

        for number, out_ref in enumerate((stay_ref, away_ref, go_ref.at[0], go_ref.at[1])):

            @pl.when(q == number)
            def _():
                store(step, slot, out_ref).start()

        return carry

    lax.fori_loop(0, steps, weights, 0)
    for step in (steps - 2, steps - 1):
        store(step, step % 2, stay_ref).wait()


def expert_rows(x, geo, here, w_ref, xt_ref, geot_ref, act_ref, gi_ref, acc_ref):
    xt_ref[:, here] = x.T
    geot_ref[:, here] = geo.T
    worth = 0.0
    for q in range(4):
        inner = dot(x, w_ref[q, :D])
        grad_active = dot(geo, w_ref[q, D:], 1, 1)
        act, slope = gelu_pair(inner)
        gi = (slope * grad_active).astype(BF)
        act_ref[q, here] = act.astype(BF)
        gi_ref[q, here] = gi
        back = dot(gi, w_ref[q, :D], 1, 1)
        if q == 0:
            acc_ref[...] = back
        else:
            acc_ref[...] += back
        worth = worth + jnp.sum(act * grad_active, axis=1, keepdims=True)
    return worth


def expert_outs(start, size, column, act_ref, w_ref):
    here = pl.ds(pl.multiple_of(start, size), size)
    cols = pl.ds(pl.multiple_of(column * TILE, TILE), TILE)
    total = None
    for q in range(4):
        term = dot(act_ref[q, here], w_ref[q, D:, cols])
        total = term if total is None else total + term
    return cols, total


def expert_kernel(
    count, cap, packed_ref, send_meta_ref, grads_ref, router_ref, w0, w1, w2, w3,
    came_ref, result_ref, stay_ref, away_ref, go_ref, grouter_ref,
    w_ref, x_ref, xt_ref, geot_ref, act_ref, gi_ref, gsend_ref, meta_ref, acc_ref, stage_ref,
    x_send, x_recv, m_send, m_recv, r_send, r_recv, local_sem, w_sem, out_sem,
):
    me = lax.axis_index("expert")
    barrier = pltpu.get_barrier_semaphore()

    def peer(k):
        return flipped(me, k, count)

    source = peer

    def greet(k, carry):
        pl.semaphore_signal(
            barrier, inc=1, device_id={"expert": peer(k)}, device_id_type=pl.DeviceIdType.MESH
        )
        return carry

    lax.fori_loop(1, count, greet, 0)
    pl.semaphore_wait(barrier, count - 1)

    def rows_of(k):
        return pl.ds(pl.multiple_of(k * cap, cap), cap)

    def send_rows(k):
        return pltpu.make_async_remote_copy(
            src_ref=packed_ref.at[rows_of(peer(k))],
            dst_ref=x_ref.at[rows_of(k)],
            send_sem=x_send.at[k],
            recv_sem=x_recv.at[k],
            device_id={"expert": peer(k)},
            device_id_type=pl.DeviceIdType.MESH,
        )

    def send_meta(k):
        return pltpu.make_async_remote_copy(
            src_ref=send_meta_ref.at[peer(k)],
            dst_ref=meta_ref.at[k],
            send_sem=m_send.at[k],
            recv_sem=m_recv.at[k],
            device_id={"expert": peer(k)},
            device_id_type=pl.DeviceIdType.MESH,
        )

    def send_back(k):
        return pltpu.make_async_remote_copy(
            src_ref=gsend_ref.at[rows_of(k)],
            dst_ref=came_ref.at[rows_of(me)],
            send_sem=r_send.at[k],
            recv_sem=r_recv.at[k],
            device_id={"expert": source(k)},
            device_id_type=pl.DeviceIdType.MESH,
        )

    def start_sends(k, carry):
        send_meta(k).start()
        send_rows(k).start()
        return carry

    lax.fori_loop(count // 2, count, start_sends, 0)
    lax.fori_loop(1, count // 2, start_sends, 0)
    own_rows = pltpu.make_async_copy(packed_ref.at[rows_of(me)], x_ref.at[rows_of(0)], local_sem.at[0])
    own_rows.start()
    own_meta = pltpu.make_async_copy(send_meta_ref.at[me], meta_ref.at[0], local_sem.at[1])
    own_meta.start()
    loads = [
        pltpu.make_async_copy(w, w_ref.at[i], w_sem.at[i]) for i, w in enumerate((w0, w1, w2, w3))
    ]
    for load in loads:
        load.start()
    grouter_ref[...] = jnp.zeros_like(grouter_ref)
    experts = router_ref.shape[1]
    own_rows.wait()
    own_meta.wait()
    for load in loads:
        load.wait()
    group = max(1, CHUNK // cap)
    span = group * cap

    def chunk(j, carry):
        for i in range(group):
            k = j * group + i

            @pl.when(k > 0)
            def _():
                send_rows(k).wait_recv()
                send_meta(k).wait_recv()

        here = pl.ds(pl.multiple_of(j * span, span), span)
        meta = jnp.concatenate([meta_ref[j * group + i].T for i in range(group)], axis=0)
        gate = meta[:, 0:1] + meta[:, 1:2] + meta[:, 2:3]
        code = meta[:, 3:4].astype(jnp.int32)
        gy = jnp.concatenate([grads_ref[rows_of(source(j * group + i)), :] for i in range(group)], axis=0)
        geo = (gate * gy.astype(F32)).astype(BF)
        x = x_ref[here, :]
        worth = expert_rows(x, geo, here, w_ref, xt_ref, geot_ref, act_ref, gi_ref, acc_ref)
        ids = iota((span, experts), 1)
        signs = (ids == me).astype(F32) - (ids + 1 == code).astype(F32)
        share = jnp.where(code > 0, (1.0 - gate) * worth, 0.0) * signs
        high = share.astype(BF)
        low = (share - high.astype(F32)).astype(BF)
        gsend_ref[here, :] = (acc_ref[...] + dot(high, router_ref[...], 1, 1)).astype(BF)
        grouter_ref[...] += dot(high.T, x) + dot(low.T, x)
        for i in range(group):
            k = j * group + i

            @pl.when(k > 0)
            def _():
                send_back(k).start()

        return carry

    lax.fori_loop(0, count // group, chunk, 0)
    own_back = pltpu.make_async_copy(gsend_ref.at[rows_of(0)], came_ref.at[rows_of(me)], local_sem.at[0])
    own_back.start()

    def results(step, carry):
        j = step // (D // TILE)
        meta = jnp.concatenate([meta_ref[j * group + i].T for i in range(group)], axis=0)
        gate = meta[:, 0:1] + meta[:, 1:2] + meta[:, 2:3]
        cols, total = expert_outs(j * span, span, lax.rem(step, D // TILE), act_ref, w_ref)
        out = (gate * total).astype(BF)
        for i in range(group):
            result_ref[rows_of(source(j * group + i)), cols] = out[i * cap : (i + 1) * cap]
        return carry

    lax.fori_loop(0, count // group * (D // TILE), results, 0)
    weight_grads(xt_ref, geot_ref, act_ref, gi_ref, stage_ref, stay_ref, away_ref, go_ref, out_sem)
    own_back.wait()

    def finish(k, carry):
        send_rows(k).wait_send()
        send_meta(k).wait_send()
        send_back(k).wait()
        return carry

    lax.fori_loop(1, count, finish, 0)


def mesh_copy(src, dst, send_sem, recv_sem, target):
    return pltpu.make_async_remote_copy(
        src_ref=src,
        dst_ref=dst,
        send_sem=send_sem,
        recv_sem=recv_sem,
        device_id={"expert": target},
        device_id_type=pl.DeviceIdType.MESH,
    )


LINE = 4


def expert_line_kernel(
    cap, normed_ref, info_in, router_ref, grads_in, near_ref, near_info_ref, up_ref, down_ref, far_up_ref, far_half_ref,
    came_ref, result_ref, stay_ref, away_ref, go_ref, grouter_ref,
    grads_ref, w_ref, block_ref, info_ref, x_ref, xs_ref, meta_ref, ms_ref, xt_ref, geot_ref, act_ref, gi_ref, acc_ref, stage_ref,
    b_send, b_recv, i_send, i_recv, x_send, x_recv, m_send, m_recv, r_send, r_recv, local_sem, w_sem, v_send, v_recv, y_send, y_recv, grads_sem, near_sem, out_sem,
):
    count = 2 * LINE
    me = lax.axis_index("expert")
    place = me // 2
    side = me - 2 * place
    mate = me + 1 - 2 * side
    barrier = pltpu.get_barrier_semaphore()

    def greet(k, carry):
        pl.semaphore_signal(
            barrier,
            inc=1,
            device_id={"expert": lax.rem(me + k, count)},
            device_id_type=pl.DeviceIdType.MESH,
        )
        return carry

    lax.fori_loop(1, count, greet, 0)
    core = flipped(lax.axis_index("tensor"), 1, 4)
    pl.semaphore_signal(
        barrier, inc=1, device_id={"tensor": core}, device_id_type=pl.DeviceIdType.MESH
    )
    away = flipped(lax.axis_index("tensor"), 2, 4)
    pl.semaphore_signal(
        barrier, inc=1, device_id={"tensor": away}, device_id_type=pl.DeviceIdType.MESH
    )
    pl.semaphore_wait(barrier, count + 1)

    def along(block, step):
        return (
            mesh_copy(
                info_ref.at[block],
                info_ref.at[block],
                i_send.at[(step + 1) // 2, block],
                i_recv.at[block],
                me + 2 * step,
            ),
            mesh_copy(
                block_ref.at[block],
                block_ref.at[block],
                b_send.at[(step + 1) // 2, block],
                b_recv.at[block],
                me + 2 * step,
            ),
        )

    def across(block):
        return (
            mesh_copy(ms_ref.at[block], meta_ref.at[1, block], m_send.at[block], m_recv.at[block], mate),
            mesh_copy(xs_ref.at[block], x_ref.at[1, block], x_send.at[block], x_recv.at[block], mate),
        )

    def rows_of(number):
        return pl.ds(pl.multiple_of(number * cap, cap), cap)

    def origin(part, block):
        return 2 * block + side + part * (1 - 2 * side)

    def give_back(part, block):
        return mesh_copy(
            x_ref.at[part, block],
            came_ref.at[rows_of(me)],
            r_send.at[part, block],
            r_recv.at[me],
            origin(part, block),
        )

    def each(pair, act):
        for one in pair:
            act(one)

    own = (
        pltpu.make_async_copy(info_in, info_ref.at[place], local_sem.at[0]),
        pltpu.make_async_copy(normed_ref, block_ref.at[place], local_sem.at[1]),
    )
    each(own, lambda c: c.start())
    rest = D // 2
    far_down = tensor_copy(down_ref.at[rest:], w_ref.at[1, D + rest :], y_send, y_recv, away)
    far_down.start()
    grads_load = pltpu.make_async_copy(grads_in, grads_ref, grads_sem)
    grads_load.start()
    near = [
        (
            pltpu.make_async_copy(near_info_ref.at[i], info_ref.at[place + 2 * i - 1], near_sem.at[i]),
            pltpu.make_async_copy(near_ref.at[i], block_ref.at[place + 2 * i - 1], near_sem.at[i + 2]),
        )
        for i in range(2)
    ]
    inside = [place > 0, place < LINE - 1]
    for i in range(2):

        @pl.when(inside[i])
        def _():
            each(near[i], lambda c: c.start())

    weights = (
        (up_ref, 0, 0, D), (down_ref, 0, D, D), (far_up_ref, 1, 0, D), (far_half_ref, 1, D, rest),
        (w_ref.at[1, D + rest :], 1, D + rest, rest),
    )

    def load(i):
        source, q, start, size = weights[i]
        return pltpu.make_async_copy(source, w_ref.at[q, start : start + size], w_sem.at[i])

    def lend(i):
        source, q, start, size = weights[i]
        return tensor_copy(source, w_ref.at[2 + q, start : start + size], v_send.at[i], v_recv.at[i], core)

    for i in range(2):

        @pl.when(inside[i])
        def _():
            each(near[i], lambda c: c.wait())

            @pl.when(inside[1 - i])
            def _():
                each(along(place + 2 * i - 1, 1 - 2 * i), lambda c: c.start())

    for i in range(4):
        load(i).start()
        lend(i).start()
    each(own, lambda c: c.wait())
    experts = router_ref.shape[0]
    rows = normed_ref.shape[0]

    def select(block):
        info = info_ref[block]
        slots = info[0:2].astype(jnp.int32)
        lines0 = meta_lines(info[2:3], info[5:6])
        lines1 = meta_lines(info[3:4], info[4:5])
        for part, expert in ((1, mate), (0, me)):
            where = iota((cap, rows), 0) + expert * cap
            pick0 = where == slots[0:1]
            pick1 = where == slots[1:2]
            taken = dot((pick0 | pick1).astype(BF), block_ref[block]).astype(BF)
            meta = dot(lines0, pick0.astype(BF), 1, 1) + dot(lines1, pick1.astype(BF), 1, 1)
            if part:
                xs_ref[block] = taken
                ms_ref[block] = meta
                each(across(block), lambda c: c.start())
            else:
                x_ref[0, block] = taken
                meta_ref[0, block] = meta

    select(place)
    grouter_ref[...] = jnp.zeros_like(grouter_ref)
    mirror = place // 2
    inward = place + mirror * (LINE - 1 - 2 * place)

    def block_at(i):
        step = i + inward * (1 - i // 2 - 2 * (i // 2 - i // (LINE - 1)))
        return step + mirror * (LINE - 1 - 2 * step)

    def chunk_at(c):
        part = lax.rem(c + 1, 2) - (7 - c) // 7 + c // 7
        return part, block_at((c + 1) // 2 - part * ((c + 1) // 2 - (c - 1) // 2))

    for i in range(2):

        @pl.when(inside[i])
        def _():
            select(place + 2 * i - 1)

    grads_load.wait()
    for i in range(4):
        load(i).wait()
        lend(i).wait_recv()
    far_down.wait_recv()
    lend(4).start()
    lend(4).wait_recv()

    def chunk(c, carry):
        for distance in range(2, LINE):

            @pl.when(c == 4 * distance - 7)
            def _():
                line_accept(place, distance, along, select)

        part, block = chunk_at(c)

        @pl.when(part == 1)
        def _():
            each(across(block), lambda c: c.wait_recv())

        here = pl.ds(pl.multiple_of(c * cap, cap), cap)
        meta = meta_ref[part, block].T
        gate = meta[:, 0:1] + meta[:, 1:2] + meta[:, 2:3]
        code = meta[:, 3:4].astype(jnp.int32)
        geo = (gate * grads_ref[part, block].astype(F32)).astype(BF)
        x = x_ref[part, block]
        worth = expert_rows(x, geo, here, w_ref, xt_ref, geot_ref, act_ref, gi_ref, acc_ref)
        ids = iota((cap, experts), 1)
        signs = (ids == me).astype(F32) - (ids + 1 == code).astype(F32)
        share = jnp.where(code > 0, (1.0 - gate) * worth, 0.0) * signs
        high = share.astype(BF)
        low = (share - high.astype(F32)).astype(BF)
        grouter_ref[...] += dot(high.T, x) + dot(low.T, x)
        x_ref[part, block] = (acc_ref[...] + dot(high, router_ref[...])).astype(BF)

        @pl.when(origin(part, block) != me)
        def _():
            give_back(part, block).start()

        return carry

    lax.fori_loop(0, count, chunk, 0)
    own_back = pltpu.make_async_copy(x_ref.at[0, place], came_ref.at[rows_of(me)], local_sem.at[0])
    own_back.start()

    def results(step, carry):
        first = step // (D // TILE) * LINE
        cols, total = expert_outs(first * cap, LINE * cap, lax.rem(step, D // TILE), act_ref, w_ref)
        for i in range(LINE):
            part, block = chunk_at(first + i)
            meta = meta_ref[part, block].T
            gate = meta[:, 0:1] + meta[:, 1:2] + meta[:, 2:3]
            result_ref[rows_of(origin(part, block)), cols] = (
                gate * total[i * cap : (i + 1) * cap]
            ).astype(BF)
        return carry

    lax.fori_loop(0, 2 * (D // TILE), results, 0)
    weight_grads(xt_ref, geot_ref, act_ref, gi_ref, stage_ref, stay_ref, away_ref, go_ref, out_sem)
    own_back.wait()
    for i in range(5):
        lend(i).wait_send()
    far_down.wait_send()
    line_sent(place, along, 1)
    for block in range(LINE):
        each(across(block), lambda c: c.wait_send())
        for part in (0, 1):

            @pl.when(origin(part, block) != me)
            def _():
                give_back(part, block).wait_send()

    for number in range(count):

        @pl.when(number != me)
        def _():
            mesh_copy(
                x_ref.at[0, 0], came_ref.at[rows_of(number)], r_send.at[0, 0], r_recv.at[number], mate
            ).wait_recv()


def turn_kernel(lengths_ref, came_ref, slots_ref, hidden_ref, gain_ref, grad_ref, gh_ref, ga_ref, gain_out):
    gn = dot(back_matrix(slots_ref, came_ref.shape[0]), came_ref[...])
    hidden = hidden_ref[...]
    scale = rms(hidden)
    unit = hidden * scale
    gain_out[...] = jnp.broadcast_to(jnp.sum(gn * unit, axis=0, keepdims=True), gain_out.shape)
    g = gn * gain_ref[...]
    valid = (iota((hidden.shape[0], 1), 0) < own_valid(lengths_ref, hidden.shape[0])).astype(F32)
    gh = scale * (g - unit * jnp.mean(g * unit, axis=1, keepdims=True)) + valid * grad_ref[...].astype(F32)
    gh_ref[...] = gh
    ga_ref[...] = gh.astype(BF)


def output_kernel(lengths_ref, came_ref, slots_ref, hidden_ref, out_ref):
    mix = dot(back_matrix(slots_ref, came_ref.shape[0]), came_ref[...])
    hidden = hidden_ref[...]
    valid = (iota((hidden.shape[0], 1), 0) < own_valid(lengths_ref, hidden.shape[0])).astype(F32)
    out_ref[...] = (valid * (hidden + mix)).astype(BF)


def last_kernel(x_ref, keep_ref, got_ref, gain_ref, gh_ref, out_ref, gain_out):
    x = x_ref[...].astype(F32)
    scale = rms(x)
    unit = x * scale
    gn = keep_ref[...] + got_ref[...].astype(F32)
    gain_out[...] = jnp.broadcast_to(jnp.sum(gn * unit, axis=0, keepdims=True), gain_out.shape)
    g = gn * gain_ref[...]
    out_ref[...] = (
        gh_ref[...] + scale * (g - unit * jnp.mean(g * unit, axis=1, keepdims=True))
    ).astype(BF)


def moe(experts, cap, packed, meta, grads, router, quarters):
    spots = experts * cap
    anyspec = pl.BlockSpec(memory_space=pl.ANY)
    dma = pltpu.SemaphoreType.DMA
    return pl.pallas_call(
        functools.partial(expert_kernel, experts, cap),
        out_shape=[
            jax.ShapeDtypeStruct((spots, D), BF),
            jax.ShapeDtypeStruct((spots, D), BF),
            jax.ShapeDtypeStruct((2 * D, D), BF),
            jax.ShapeDtypeStruct((2 * D, D), BF),
            jax.ShapeDtypeStruct((2, 2 * D, D), BF),
            jax.ShapeDtypeStruct((experts, D), F32),
        ],
        in_specs=[anyspec, VM, VM, VM] + [anyspec] * 4,
        out_specs=[anyspec, VM, anyspec, anyspec, anyspec, VM],
        scratch_shapes=[
            pltpu.VMEM((4, 2 * D, D), BF),
            pltpu.VMEM((spots, D), BF),
            pltpu.VMEM((D, spots), BF),
            pltpu.VMEM((D, spots), BF),
            pltpu.VMEM((4, spots, D), BF),
            pltpu.VMEM((4, spots, D), BF),
            pltpu.VMEM((spots, D), BF),
            pltpu.VMEM((experts, 8, cap), F32),
            pltpu.VMEM((CHUNK, D), F32),
            pltpu.VMEM((2, D, TILE), BF),
            dma((experts,)),
            dma((experts,)),
            dma((experts,)),
            dma((experts,)),
            dma((experts,)),
            dma((experts,)),
            dma((2,)),
            dma((4,)),
            dma((2,)),
        ],
        compiler_params=pltpu.CompilerParams(
            collective_id=1, has_side_effects=True, vmem_limit_bytes=60 * MIB
        ),
        cost_estimate=pl.CostEstimate(flops=12 * spots * D * 4 * D, bytes_accessed=60 * MIB, transcendentals=0),
        name="experts",
    )(packed, meta, grads, router, *quarters)


def moe_line(experts, cap, normed, info, router, others):
    rows = normed.shape[0]
    spots = experts * cap
    anyspec = pl.BlockSpec(memory_space=pl.ANY)
    dma = pltpu.SemaphoreType.DMA
    return pl.pallas_call(
        functools.partial(expert_line_kernel, cap),
        out_shape=[
            jax.ShapeDtypeStruct((spots, D), BF),
            jax.ShapeDtypeStruct((spots, D), BF),
            jax.ShapeDtypeStruct((2 * D, D), BF),
            jax.ShapeDtypeStruct((2 * D, D), BF),
            jax.ShapeDtypeStruct((2, 2 * D, D), BF),
            jax.ShapeDtypeStruct((experts, D), F32),
        ],
        in_specs=[VM, VM, VM] + [anyspec] * 7,
        out_specs=[anyspec, VM, anyspec, anyspec, anyspec, VM],
        scratch_shapes=[
            pltpu.VMEM((2, LINE, cap, D), BF),
            pltpu.VMEM((4, 2 * D, D), BF),
            pltpu.VMEM((LINE, rows, D), BF),
            pltpu.VMEM((LINE, 8, rows), F32),
            pltpu.VMEM((2, LINE, cap, D), BF),
            pltpu.VMEM((LINE, cap, D), BF),
            pltpu.VMEM((2, LINE, 8, cap), F32),
            pltpu.VMEM((LINE, 8, cap), F32),
            pltpu.VMEM((D, spots), BF),
            pltpu.VMEM((D, spots), BF),
            pltpu.VMEM((4, spots, D), BF),
            pltpu.VMEM((4, spots, D), BF),
            pltpu.VMEM((cap, D), F32),
            pltpu.VMEM((2, D, TILE), BF),
            dma((2, LINE)),
            dma((LINE,)),
            dma((2, LINE)),
            dma((LINE,)),
            dma((LINE,)),
            dma((LINE,)),
            dma((LINE,)),
            dma((LINE,)),
            dma((2, LINE)),
            dma((experts,)),
            dma((2,)),
            dma((4,)),
            dma((5,)),
            dma((5,)),
            dma,
            dma,
            dma,
            dma((4,)),
            dma((2,)),
        ],
        compiler_params=pltpu.CompilerParams(
            collective_id=2, has_side_effects=True, vmem_limit_bytes=62 * MIB
        ),
        cost_estimate=pl.CostEstimate(flops=12 * spots * D * 4 * D, bytes_accessed=60 * MIB, transcendentals=0),
        name="experts_line",
    )(normed, info, router, *others)


def tensor_copy(src, dst, send_sem, recv_sem, target):
    return pltpu.make_async_remote_copy(
        src_ref=src,
        dst_ref=dst,
        send_sem=send_sem,
        recv_sem=recv_sem,
        device_id={"tensor": target},
        device_id_type=pl.DeviceIdType.MESH,
    )


def sums(
    pair_done, beside, gw_ref, pair_ref, keep_ref, send_ref, x_in, gain_ref, gh_ref, moe_ref, router_ref, bias0_ref, bias1_ref,
    gwt_out, gow_out, gin_out, attn_out, moe_out, router_out, bias_out,
    small_out, part_ref, cross_ref, line_ref, from_ref, all_ref, got_ref, lines_ref, few_ref, ranks_ref,
    a_send, a_recv, b_send, b_recv, c_send, c_recv, d_send, d_recv, s_send, s_recv, f_send, f_recv, t_send, t_recv, g_send, g_recv,
):
    count = 2 * LINE
    me = lax.axis_index("expert")
    rank = lax.axis_index("tensor")
    place = me // 2
    side = me - 2 * place
    mate = me + 1 - 2 * side
    size = part_ref.shape[0] // count
    def slab(which, number):
        return pl.ds(pl.multiple_of((which * LINE + number) * size, size), size)

    swap = tensor_copy(send_ref, got_ref, s_send, s_recv, flipped(rank, 1, 4))
    swap.start()
    pair_done()
    part_ref[...] = (gw_ref[...] + pair_ref[...].astype(F32)).astype(BF)
    rows = gwt_out.shape[0]

    def cross(number):
        return mesh_copy(
            part_ref.at[slab(1 - side, number)], cross_ref.at[number], a_send.at[number], a_recv.at[number], mate
        )

    def along(number):
        return mesh_copy(
            line_ref.at[number], from_ref.at[place], b_send.at[number], b_recv.at[place], 2 * number + side
        )

    def spread(number):
        return mesh_copy(
            all_ref.at[slab(side, place)],
            all_ref.at[slab(side, place)],
            c_send.at[number],
            c_recv.at[place],
            2 * number + side,
        )

    def over(number):
        return mesh_copy(
            all_ref.at[slab(side, number)], all_ref.at[slab(side, number)], d_send.at[number], d_recv.at[number], mate
        )

    for number in range(LINE):
        cross(number).start()

    swap.wait()
    x = x_in[...].astype(F32)
    scale = rms(x)
    unit = x * scale
    gn = keep_ref[...] + got_ref[...].astype(F32)
    attn = jnp.sum(gn * unit, axis=0, keepdims=True)
    g = gn * gain_ref[...]
    gin_out[...] = (gh_ref[...] + scale * (g - unit * jnp.mean(g * unit, axis=1, keepdims=True))).astype(BF)

    heads = gow_out.shape[0] // HD
    blank = jnp.zeros((1, 128), F32)

    def flat(bias_ref):
        line = [bias_ref[h : h + 1, :NB] for h in range(heads)]
        return jnp.concatenate(line + [jnp.zeros((1, 128 - heads * NB), F32)], axis=1)

    own_bias, pair_bias = flat(bias0_ref), flat(bias1_ref)
    other = flipped(rank, 2, 4)
    for j in range(D // 128):
        lines_ref[j] = router_ref[:, j * 128 : (j + 1) * 128]
    for j, row in ((6, attn), (7, moe_ref[0:1])):
        places = [2 * (j - 6), 2 * (j - 6) + 1]
        bias = [
            jnp.where(rank == p, own_bias, blank) + jnp.where(other == p, pair_bias, blank) for p in places
        ]
        lines_ref[j] = jnp.concatenate([row[:, i * 128 : (i + 1) * 128] for i in range(6)] + bias, axis=0)

    def small(k):
        return mesh_copy(
            lines_ref.at[flipped(me, k, count)], few_ref.at[k], f_send.at[k], f_recv.at[k], flipped(me, k, count)
        )

    def rank_copy(k):
        return tensor_copy(
            ranks_ref.at[rank], ranks_ref.at[rank], t_send.at[k], t_recv.at[k], flipped(rank, k, 4)
        )

    def rank_from(k):
        return tensor_copy(
            ranks_ref.at[rank], ranks_ref.at[flipped(rank, k, 4)], t_send.at[k], t_recv.at[k], flipped(rank, k, 4)
        )

    def small_spread(k):
        return mesh_copy(
            small_out.at[me], small_out.at[me], g_send.at[k], g_recv.at[k], flipped(me, k, count)
        )

    def small_from(k):
        return mesh_copy(
            small_out.at[me], small_out.at[flipped(me, k, count)], g_send.at[k], g_recv.at[k], flipped(me, k, count)
        )

    for k in range(1, count):
        small(k).start()

    for number in range(LINE):

        @pl.when(number != place)
        def _():
            cross(number).wait_recv()
            line_ref[number] = (
                part_ref[slab(side, number)].astype(F32) + cross_ref[number].astype(F32)
            ).astype(BF)
            along(number).start()

    total = lines_ref[me]
    for k in range(1, count):
        small(k).wait_recv()
        total = total + few_ref[k]
    ranks_ref[rank] = total
    for k in range(1, 4):
        rank_copy(k).start()

    for number in range(LINE):

        @pl.when(number == place)
        def _():
            cross(number).wait_recv()

    beside()
    whole = part_ref[slab(side, place)].astype(F32) + cross_ref[place].astype(F32)
    from_ref[place] = whole.astype(BF)
    for k in range(1, LINE):
        number = lax.rem(place + k, LINE)
        mesh_copy(
            line_ref.at[number], from_ref.at[number], b_send.at[number], b_recv.at[number], mate
        ).wait_recv()
        whole = whole + from_ref[number].astype(F32)
    all_ref[slab(side, place)] = whole.astype(BF)
    over(place).start()
    for number in range(LINE):

        @pl.when(number != place)
        def _():
            spread(number).start()

    for k in range(1, 4):
        rank_from(k).wait_recv()
    small_out[me] = ranks_ref[0] + ranks_ref[1] + ranks_ref[2] + ranks_ref[3]
    for k in range(1, count):
        small_spread(k).start()

    for k in range(1, LINE):
        number = lax.rem(place + k, LINE)
        mesh_copy(
            all_ref.at[slab(side, number)], all_ref.at[slab(side, number)], c_send.at[number], c_recv.at[number], mate
        ).wait_recv()
        over(number).start()
    for k in range(1, count):
        small_from(k).wait_recv()
    for number in range(LINE):
        mesh_copy(
            all_ref.at[slab(1 - side, number)],
            all_ref.at[slab(1 - side, number)],
            d_send.at[number],
            d_recv.at[number],
            mate,
        ).wait_recv()
    attn_out[...] = jnp.concatenate([small_out[6, i : i + 1] for i in range(6)], axis=1)
    moe_out[...] = jnp.concatenate([small_out[7, i : i + 1] for i in range(6)], axis=1)
    router_out[...] = jnp.concatenate([small_out[j] for j in range(D // 128)], axis=1)
    bias = functools.reduce(
        jnp.add,
        [jnp.where(rank == p, small_out[6 + p // 2, 6 + p % 2 : 7 + p % 2], blank) for p in range(4)],
    )
    bias_out[...] = jnp.concatenate([bias[:, h * NB : (h + 1) * NB] for h in range(heads)], axis=0)
    gwt_out[...] = all_ref[:rows].astype(F32)
    gow_out[...] = all_ref[rows:].astype(F32)
    for number in range(LINE):
        cross(number).wait_send()
        over(number).wait_send()

        @pl.when(number != place)
        def _():
            along(number).wait_send()
            spread(number).wait_send()

    for k in range(1, count):
        small(k).wait_send()
        small_spread(k).wait_send()
    for k in range(1, 4):
        rank_copy(k).wait_send()


PARTS = 6


def finish_kernel(
    heads, cap, lengths_ref,
    table0_ref, table1_ref, came_ref, slots_ref, hidden_ref, gain2_ref, grad_ref, gain1_ref, router_ref,
    result_in, go_in, away_in, x_in, normed_in, wt_in, ow_in, pw_in, qkvt0_in, mixt0_in, lse0_in, qkvt1_in, mixt1_in, lse1_in,
    out_ref, gin_out, gwt_out, gow_out, attn_out, moe_out, router_out, bias_out, came_go_ref, came_away_ref,
    outs_ref, gorecv_ref, away_ref, x_ref, normed_ref, wt_ref, ow_ref, pw_ref, qkvt0_ref, mixt0_ref, lse0_ref, qkvt1_ref, mixt1_ref, lse1_ref,
    gh_ref, ga_ref, other_ref, moe_ref, gpart_ref, gpair_ref, gown_ref, bias0_ref, bias1_ref, keep_ref, send_ref,
    all_ga_ref, got_ref, gt_ref, d0_ref, d1_ref, npart_ref,
    o_send, o_recv, v_send, v_recv, y_send, y_recv, w_send, w_recv, e_send, e_recv, load_sem, *tail_refs,
):
    count = 2 * LINE
    me = lax.axis_index("expert")
    rank = lax.axis_index("tensor")
    core = flipped(rank, 1, 4)
    away_rank = flipped(rank, 2, 4)
    barrier = pltpu.get_barrier_semaphore()
    for k in range(1, count):
        pl.semaphore_signal(
            barrier, inc=1, device_id={"expert": flipped(me, k, count)}, device_id_type=pl.DeviceIdType.MESH
        )
    for k in range(1, 4):
        pl.semaphore_signal(
            barrier, inc=1, device_id={"tensor": flipped(rank, k, 4)}, device_id_type=pl.DeviceIdType.MESH
        )
    pl.semaphore_wait(barrier, count + 2)

    def rows_of(number):
        return pl.ds(pl.multiple_of(number * cap, cap), cap)

    def result(k):
        return mesh_copy(
            result_in.at[rows_of(flipped(me, k, count))],
            outs_ref.at[rows_of(me)],
            o_send.at[k],
            o_recv.at[k],
            flipped(me, k, count),
        )

    order = list(range(LINE, count)) + list(range(1, LINE))
    for k in order:
        result(k).start()
    own_result = pltpu.make_async_copy(result_in.at[rows_of(me)], outs_ref.at[rows_of(me)], load_sem.at[0])
    own_result.start()
    away_load = pltpu.make_async_copy(away_in, away_ref, load_sem.at[1])
    away_load.start()
    go_away = tensor_copy(go_in.at[1], gorecv_ref, v_send.at[0], v_recv.at[0], core)
    go_away.start()
    go_stay = tensor_copy(go_in.at[0], came_go_ref, v_send.at[1], v_recv.at[1], core)
    places = (
        (normed_in, normed_ref),
        (pw_in, pw_ref),
        (qkvt1_in, qkvt1_ref),
        (mixt1_in, mixt1_ref),
        (lse1_in, lse1_ref),
        (wt_in, wt_ref),
        (ow_in, ow_ref),
        (qkvt0_in, qkvt0_ref),
        (mixt0_in, mixt0_ref),
        (lse0_in, lse0_ref),
        (x_in, x_ref),
    )
    loads = [pltpu.make_async_copy(a, b, load_sem.at[i + 2]) for i, (a, b) in enumerate(places)]
    for load in loads:
        load.start()

    turn_kernel(lengths_ref, came_ref, slots_ref, hidden_ref, gain2_ref, grad_ref, gh_ref, ga_ref, moe_ref)
    ga_swap = tensor_copy(ga_ref, other_ref, w_send, w_recv, core)
    ga_swap.start()
    away_load.wait()
    go_away.wait_recv()
    size = away_ref.shape[0] // PARTS

    def lines(i):
        return pl.ds(i * size, size)

    def away(i):
        return tensor_copy(
            away_ref.at[lines(i)], came_away_ref.at[lines(i)], y_send.at[i], y_recv.at[i], away_rank
        )

    for i in range(PARTS):
        away_ref[lines(i)] = (
            away_ref[lines(i)].astype(F32) + gorecv_ref[lines(i)].astype(F32)
        ).astype(BF)
        if i < 2:
            away(i).start()
    ga_swap.wait()
    go_stay.start()
    for load in loads:
        load.wait()
    inner = heads * HD
    attn_bwd_kernel(
        False, heads, lengths_ref, table1_ref,
        normed_ref, pw_ref.at[: 3 * inner], pw_ref.at[3 * inner :], qkvt1_ref, mixt1_ref, lse1_ref, ga_ref, other_ref,
        gpart_ref, bias1_ref, npart_ref, all_ga_ref, got_ref, gt_ref, d0_ref, d1_ref,
    )
    pair = tensor_copy(gpart_ref, gpair_ref, e_send, e_recv, away_rank)
    pair.start()
    attn_bwd_kernel(
        True, heads, lengths_ref, table0_ref,
        normed_ref, wt_ref, ow_ref, qkvt0_ref, mixt0_ref, lse0_ref, ga_ref, other_ref, npart_ref,
        gown_ref, bias0_ref, keep_ref, send_ref, all_ga_ref, got_ref, gt_ref, d0_ref, d1_ref, npart_ref,
    )

    def pair_done():
        pair.wait_recv()
        for i in range(2, PARTS):
            away(i).start()

    def beside():
        own_result.wait()
        for k in order:
            result(k).wait_recv()
        output_kernel(lengths_ref, outs_ref, slots_ref, hidden_ref, out_ref)

    sums(
        pair_done, beside, gown_ref, gpair_ref, keep_ref, send_ref, x_ref, gain1_ref, gh_ref, moe_ref, router_ref,
        bias0_ref, bias1_ref, gwt_out, gow_out, gin_out, attn_out, moe_out, router_out, bias_out, *tail_refs,
    )
    for k in order:
        result(k).wait_send()
    pair.wait_send()
    go_away.wait_send()
    go_stay.wait()
    for i in range(PARTS):
        away(i).wait()


def finish(heads, cap, scalars, arrays, others):
    dma = pltpu.SemaphoreType.DMA
    count = 2 * LINE
    spots = count * cap
    rows = arrays[4].shape[0]
    local = heads * HD
    part = 4 * local // count
    anyspec = pl.BlockSpec(memory_space=pl.ANY)
    half = (rows, D)
    tail_sems = [dma((LINE,))] * 8 + [dma, dma] + [dma((count,))] * 2 + [dma((4,))] * 2 + [dma((count,))] * 2
    shapes = [
        ((spots, D), BF), ((2 * D, D), BF), ((2 * D, D), BF), (half, BF), ((SEQ, D), BF), ((3 * local, D), BF),
        ((local, D), BF), ((4 * local, D), BF), ((3 * local, SEQ), BF), ((local, SEQ), BF), ((8, SEQ), F32),
        ((3 * local, SEQ), BF), ((local, SEQ), BF), ((8, SEQ), F32),
        (half, F32), (half, BF), (half, BF), ((8, D), F32), ((4 * local, D), BF), ((4 * local, D), BF),
        ((4 * local, D), F32), ((8, 128), F32), ((8, 128), F32), (half, F32), (half, BF),
        ((SEQ, D), BF), ((local, SEQ), BF), ((3 * local, SEQ), BF), ((TILE, TILE), F32), ((TILE, TILE), F32), ((SEQ, D), F32),
    ]
    tail_shapes = [
        ((count, 8, 128), F32),
        ((4 * local, D), BF), ((LINE, part, D), BF), ((LINE, part, D), BF), ((LINE, part, D), BF), ((4 * local, D), BF),
        (half, BF), ((count, 8, 128), F32), ((count, 8, 128), F32), ((4, 8, 128), F32),
    ]
    return pl.pallas_call(
        functools.partial(finish_kernel, heads, cap),
        out_shape=[
            jax.ShapeDtypeStruct(half, BF),
            jax.ShapeDtypeStruct(half, BF),
            jax.ShapeDtypeStruct((3 * local, D), F32),
            jax.ShapeDtypeStruct((local, D), F32),
            jax.ShapeDtypeStruct((1, D), F32),
            jax.ShapeDtypeStruct((1, D), F32),
            jax.ShapeDtypeStruct((count, D), F32),
            jax.ShapeDtypeStruct((heads, NB), F32),
            jax.ShapeDtypeStruct((2 * D, D), BF),
            jax.ShapeDtypeStruct((2 * D, D), BF),
        ],
        in_specs=[SM] * len(scalars) + [VM] * len(arrays) + [anyspec] * len(others),
        out_specs=[VM] * 8 + [anyspec] * 2,
        scratch_shapes=[pltpu.VMEM(*v) for v in shapes]
        + [dma((count,)), dma((count,)), dma((2,)), dma((2,)), dma((PARTS,)), dma((PARTS,)), dma, dma, dma, dma, dma((16,))]
        + [pltpu.VMEM(*v) for v in tail_shapes]
        + tail_sems,
        compiler_params=pltpu.CompilerParams(
            collective_id=3, has_side_effects=True, vmem_limit_bytes=62 * MIB
        ),
        cost_estimate=pl.CostEstimate(flops=0, bytes_accessed=200 * MIB, transcendentals=0),
        name="finish",
    )(*scalars, *arrays, *others)


def line_accept(place, distance, copies, take):
    for step in (-1, 1):
        block = place + step * distance

        @pl.when((block >= 0) & (block < LINE))
        def _():
            for one in copies(block, -step):
                one.wait_recv()
            ahead = place - step

            @pl.when((ahead >= 0) & (ahead < LINE))
            def _():
                for one in copies(block, -step):
                    one.start()

    for step in (-1, 1):
        block = place + step * distance

        @pl.when((block >= 0) & (block < LINE))
        def _():
            take(block)


def line_sent(place, copies, least):
    for block in range(LINE):
        for step in (-1, 1):

            @pl.when((place + step >= 0) & (place + step < LINE) & ((place - block) * step >= least))
            def _():
                for one in copies(block, step):
                    one.wait_send()


def begin_kernel(
    heads, cap, lengths_ref,
    table_ref, x_ref, gain1_ref, wt_ref, ow_ref, routes_ref, grad_ref, router_ref, gain2_ref, up_ref, down_ref,
    normed_out, qkvt0_out, mixt0_out, lse0_out, qkvt1_out, mixt1_out, lse1_out, hidden_ref, normed2_ref, info_ref, slots_ref,
    pw_ref, table1_ref, gy_ref, far_up_ref, far_half_ref, near_ref, near_info_ref,
    other_ref, got_ref, part_ref, keep_ref, send_ref, block_ref, places_ref, gsend_ref, gkeep_ref,
    normed_ref, qkvt0_ref, mixt0_ref, lse0_ref, qkvt1_ref, mixt1_ref, lse1_ref,
    b_send, b_recv, i_send, i_recv, x_send, x_recv, v_send, v_recv, y_send, y_recv, n_send, n_recv, keep_sem, store_sem,
):
    count = 2 * LINE
    me = lax.axis_index("expert")
    rank = lax.axis_index("tensor")
    place = me // 2
    side = me - 2 * place
    mate = me + 1 - 2 * side
    core = flipped(rank, 1, 4)
    away = flipped(rank, 2, 4)
    inner = heads * HD
    barrier = pltpu.get_barrier_semaphore()
    for k in range(1, count):
        pl.semaphore_signal(
            barrier, inc=1, device_id={"expert": flipped(me, k, count)}, device_id_type=pl.DeviceIdType.MESH
        )
    for target in (core, away):
        pl.semaphore_signal(
            barrier, inc=1, device_id={"tensor": target}, device_id_type=pl.DeviceIdType.MESH
        )
    pl.semaphore_wait(barrier, count + 1)

    swap = tensor_copy(x_ref, other_ref, v_send.at[0], v_recv.at[0], core)
    swap.start()
    pair = (
        tensor_copy(ow_ref, pw_ref.at[3 * inner :], y_send.at[0], y_recv.at[0], away),
        tensor_copy(wt_ref, pw_ref.at[: 3 * inner], y_send.at[1], y_recv.at[1], away),
        tensor_copy(table_ref, table1_ref, y_send.at[2], y_recv.at[2], away),
    )
    for one in pair:
        one.start()
    far = (
        tensor_copy(up_ref, far_up_ref, y_send.at[3], y_recv.at[3], away),
        tensor_copy(down_ref.at[: D // 2], far_half_ref, y_send.at[4], y_recv.at[4], away),
    )

    def along(block, step):
        return (
            mesh_copy(
                places_ref.at[block], places_ref.at[block], i_send.at[(step + 1) // 2, block], i_recv.at[block], me + 2 * step
            ),
            mesh_copy(
                block_ref.at[block], block_ref.at[block], b_send.at[(step + 1) // 2, block], b_recv.at[block], me + 2 * step
            ),
        )

    def across(block):
        return mesh_copy(gsend_ref.at[block], gy_ref.at[1, block], x_send.at[block], x_recv.at[block], mate)

    def keep(block):
        return pltpu.make_async_copy(gkeep_ref.at[block], gy_ref.at[0, block], keep_sem.at[block])

    rows = grad_ref.shape[0]

    def take(block):
        slots = places_ref[block, 0:2].astype(jnp.int32)
        for part, expert in ((1, mate), (0, me)):
            where = iota((cap, rows), 0) + expert * cap
            picks = ((where == slots[0:1]) | (where == slots[1:2])).astype(BF)
            taken = dot(picks, block_ref[block]).astype(BF)
            if part:
                gsend_ref[block] = taken
                across(block).start()
            else:
                gkeep_ref[block] = taken
                keep(block).start()

    block_ref[place] = grad_ref[...]
    slots_kernel(count, cap, lengths_ref, routes_ref, slots_ref)
    places_ref[place] = slots_ref[...]
    for step in (-1, 1):

        @pl.when((place + step >= 0) & (place + step < LINE))
        def _():
            for one in along(place, step):
                one.start()

    take(place)
    swap.wait()
    attn_fwd_kernel(
        True, heads, lengths_ref, table_ref, x_ref, other_ref, gain1_ref, wt_ref, ow_ref,
        normed_ref, qkvt0_ref, mixt0_ref, lse0_ref, part_ref,
    )
    first = (
        (normed_ref, normed_out), (qkvt0_ref, qkvt0_out), (mixt0_ref, mixt0_out), (lse0_ref, lse0_out),
    )
    second = ((qkvt1_ref, qkvt1_out), (mixt1_ref, mixt1_out), (lse1_ref, lse1_out))
    stores = [pltpu.make_async_copy(a, b, store_sem.at[i]) for i, (a, b) in enumerate(first + second)]
    for store in stores[:4]:
        store.start()
    line_accept(place, 1, along, take)
    for one in pair:
        one.wait_recv()
    for one in far:
        one.start()
    attn_fwd_kernel(
        False, heads, lengths_ref, table1_ref, normed_ref, pw_ref.at[: 3 * inner], pw_ref.at[3 * inner :], part_ref,
        qkvt1_ref, mixt1_ref, lse1_ref, keep_ref, send_ref, part_ref,
    )
    back = tensor_copy(send_ref, got_ref, v_send.at[1], v_recv.at[1], core)
    back.start()
    for store in stores[4:]:
        store.start()
    line_accept(place, 2, along, take)
    back.wait()
    middle_line_kernel(
        count, x_ref, keep_ref, got_ref, gain2_ref, router_ref, routes_ref, slots_ref, hidden_ref, normed2_ref, info_ref
    )
    inside = [place > 0, place < LINE - 1]

    def neighbour(i):
        target = me + 2 * (1 - 2 * i)
        return (
            mesh_copy(info_ref, near_info_ref.at[i], n_send.at[i], n_recv.at[i], target),
            mesh_copy(normed2_ref, near_ref.at[i], n_send.at[i + 2], n_recv.at[i + 2], target),
        )

    for i in range(2):

        @pl.when(inside[1 - i])
        def _():
            for one in neighbour(i):
                one.start()

    line_accept(place, 3, along, take)
    for block in range(LINE):
        keep(block).wait()
        across(block).wait()
    line_sent(place, along, 0)
    for store in stores:
        store.wait()
    for one in pair:
        one.wait_send()
    for one in far:
        one.wait()
    for i in range(2):

        @pl.when(inside[i])
        def _():
            for one in neighbour(1 - i):
                one.wait_send()
            for one in neighbour(i):
                one.wait_recv()


def begin(heads, cap, scalars, arrays, others):
    dma = pltpu.SemaphoreType.DMA
    rows = arrays[1].shape[0]
    local = heads * HD
    anyspec = pl.BlockSpec(memory_space=pl.ANY)
    half = (rows, D)
    kept = [
        ((SEQ, D), BF), ((3 * local, SEQ), BF), ((local, SEQ), BF), ((8, SEQ), F32),
        ((3 * local, SEQ), BF), ((local, SEQ), BF), ((8, SEQ), F32),
    ]
    outs = kept + [
        (half, F32), (half, BF), ((8, rows), F32), ((8, rows), F32), ((4 * local, D), BF), ((heads, NB), F32),
        ((2, LINE, cap, D), BF), ((D, D), BF), ((D // 2, D), BF), ((2, rows, D), BF), ((2, 8, rows), F32),
    ]
    shapes = [
        (half, BF), (half, BF), ((SEQ, D), F32), (half, F32), (half, BF), ((LINE, rows, D), BF), ((LINE, 8, rows), F32),
        ((LINE, cap, D), BF), ((LINE, cap, D), BF),
    ] + kept
    return pl.pallas_call(
        functools.partial(begin_kernel, heads, cap),
        out_shape=[jax.ShapeDtypeStruct(*v) for v in outs],
        in_specs=[SM] * len(scalars) + [VM] * len(arrays) + [anyspec] * len(others),
        out_specs=[anyspec] * 7 + [VM] * 6 + [anyspec] * 5,
        scratch_shapes=[pltpu.VMEM(*v) for v in shapes]
        + [dma((2, LINE)), dma((LINE,)), dma((2, LINE)), dma((LINE,)), dma((LINE,)), dma((LINE,))]
        + [dma((2,)), dma((2,)), dma((5,)), dma((5,)), dma((4,)), dma((4,)), dma((LINE,)), dma((7,))],
        compiler_params=pltpu.CompilerParams(
            collective_id=4, has_side_effects=True, vmem_limit_bytes=56 * MIB
        ),
        cost_estimate=pl.CostEstimate(flops=0, bytes_accessed=200 * MIB, transcendentals=0),
        name="begin",
    )(*scalars, *arrays, *others)


def shards(
    inputs,
    lengths,
    routes,
    attn_gain,
    qkv_weight,
    out_weight,
    rel_bias,
    moe_gain,
    router_weight,
    up_weight,
    down_weight,
    out_grad,
):
    rows = inputs.shape[0]
    rank = lax.axis_index("tensor")
    expert = lax.axis_index("expert")
    heads = rel_bias.shape[1]
    inner = heads * HD
    experts = router_weight.shape[1]
    cap = 4 * rows // experts
    spots = experts * cap
    table = jnp.transpose(rel_bias)

    def swap(x, bit):
        return lax.ppermute(x, "tensor", [(i, i ^ bit) for i in range(4)])

    gain1 = attn_gain.reshape(1, D)
    gain2 = moe_gain.reshape(1, D)
    wt = jnp.transpose(qkv_weight.reshape(D, 3 * inner))
    routes_t = jnp.transpose(routes)
    up, down = up_weight[0], down_weight[0]
    line = experts == 2 * LINE and cap == TILE
    if line:
        router_t = jnp.transpose(router_weight)
        (
            normed, qkvt0, mixt0, lse0, qkvt1, mixt1, lse1, hidden, normed_two, info, slots, pair_w, pair_table, grads_in, far_up, far_half, near, near_info,
        ) = begin(
            heads,
            cap,
            (lengths,),
            (table, inputs, gain1, wt, out_weight, routes_t, out_grad, router_t, gain2),
            (up, down),
        )
        came, result, stay, away, go, grad_router = moe_line(
            experts, cap, normed_two, info, router_t, (grads_in, near, near_info, up, down, far_up, far_half)
        )
    else:
        other = swap(inputs, 1)
        pair_w = swap(jnp.concatenate([wt, out_weight], axis=0), 2)
        pair_table = swap(table, 2)

        packed_grad, slots = call(
            functools.partial(route_kernel, experts, cap),
            [((spots, D), BF), ((8, rows), F32)],
            (lengths, routes_t, out_grad),
            [SM, VM, VM],
            flops=2 * spots * rows * D,
            moved=4 * MIB,
            name="route",
        )

        def exchange(x):
            return lax.all_to_all(
                x.reshape(experts, cap, x.shape[-1]), "expert", split_axis=0, concat_axis=0, tiled=True
            ).reshape(x.shape)

        grads_in = exchange(packed_grad)
        up, down, pair_w, pair_table = lax.optimization_barrier((up, down, pair_w, pair_table))
        far_up, far_down = swap(up, 2), swap(down, 2)

        attn_cost = dict(
            flops=2 * SEQ * D * 4 * inner + heads * SEQ * SEQ * 160, moved=6 * MIB, exps=heads * SEQ * SEQ
        )
        normed, qkvt0, mixt0, lse0, part0 = call(
            functools.partial(attn_fwd_kernel, True, heads),
            [((SEQ, D), BF), ((3 * inner, SEQ), BF), ((inner, SEQ), BF), ((8, SEQ), F32), ((SEQ, D), F32)],
            (lengths, table, inputs, other, gain1, wt, out_weight),
            [SM] + [VM] * 1 + [VM] * 5,
            name="attend_own",
            **attn_cost,
        )
        wt1, ow1 = pair_w[: 3 * inner], pair_w[3 * inner :]
        qkvt1, mixt1, lse1, keep, send = call(
            functools.partial(attn_fwd_kernel, False, heads),
            [((3 * inner, SEQ), BF), ((inner, SEQ), BF), ((8, SEQ), F32), ((rows, D), F32), ((rows, D), BF)],
            (lengths, pair_table, normed, wt1, ow1, part0),
            [SM] + [VM] * 1 + [VM] * 4,
            scratch=[pltpu.VMEM((SEQ, D), F32)],
            name="attend_pair",
            **attn_cost,
        )
        got = swap(send, 1)
        middle_args = (inputs, keep, got, gain2, jnp.transpose(router_weight), routes_t, slots)
        mine = jnp.concatenate([up, down], axis=0)
        far = jnp.concatenate([far_up, far_down], axis=0)
        quarters = [mine, far, swap(mine, 1), swap(far, 1)]
        hidden, packed_rows, meta = call(
            functools.partial(middle_kernel, experts, cap),
            [((rows, D), F32), ((spots, D), BF), ((experts, 8, cap), F32)],
            middle_args,
            flops=2 * spots * rows * D,
            moved=8 * MIB,
            name="middle",
        )
        came, result, stay, away, go, grad_router = moe(
            experts, cap, packed_rows, meta, grads_in, router_weight, quarters
        )
    if line:
        outputs, grad_inputs, gwt, gow, attn_sum, moe_sum, router_sum, bias_sum, go_stay, came_away = finish(
            heads,
            cap,
            (lengths,),
            (table, pair_table, came, slots, hidden, gain2, out_grad, gain1, grad_router),
            (result, go, away, inputs, normed, wt, out_weight, pair_w, qkvt0, mixt0, lse0, qkvt1, mixt1, lse1),
        )
    else:
        came_out = exchange(result)
        came_go = swap(go, 1)
        grad_hidden, grad_attended, moe_part = call(
            turn_kernel,
            [((rows, D), F32), ((rows, D), BF), ((8, D), F32)],
            (lengths, came, slots, hidden, gain2, out_grad),
            [SM] + [VM] * 5,
            flops=2 * spots * rows * D,
            moved=8 * MIB,
            name="turn",
        )
        other_grad = swap(grad_attended, 1)
        away = (away.astype(F32) + came_go[1].astype(F32)).astype(BF)
        bwd_cost = dict(
            flops=2 * SEQ * D * 10 * inner + heads * SEQ * SEQ * 400, moved=9 * MIB, exps=heads * SEQ * SEQ
        )
        work = [
            pltpu.VMEM((SEQ, D), BF),
            pltpu.VMEM((inner, SEQ), BF),
            pltpu.VMEM((3 * inner, SEQ), BF),
            pltpu.VMEM((TILE, TILE), F32),
            pltpu.VMEM((TILE, TILE), F32),
        ]
        gpart, gbias1, npart = call(
            functools.partial(attn_bwd_kernel, False, heads),
            [((4 * inner, D), BF), ((8, 128), F32), ((SEQ, D), F32)],
            (lengths, pair_table, normed, wt1, ow1, qkvt1, mixt1, lse1, grad_attended, other_grad),
            [SM] + [VM] * 1 + [VM] * 8,
            scratch=work,
            name="attend_pair_back",
            **bwd_cost,
        )
        gpair = swap(gpart, 2)
        gown, gbias0, keep_n, send_n = call(
            functools.partial(attn_bwd_kernel, True, heads),
            [((4 * inner, D), F32), ((8, 128), F32), ((rows, D), F32), ((rows, D), BF)],
            (lengths, table, normed, wt, out_weight, qkvt0, mixt0, lse0, grad_attended, other_grad, npart),
            [SM] + [VM] * 1 + [VM] * 9,
            scratch=work + [pltpu.VMEM((SEQ, D), F32)],
            name="attend_own_back",
            **bwd_cost,
        )
        away, gpair, gown = lax.optimization_barrier((away, gpair, gown))
        came_away = swap(away, 2)
        got_n = swap(send_n, 1)
        grad_inputs, attn_part = call(
            last_kernel,
            [((rows, D), BF), ((8, D), F32)],
            (inputs, keep_n, got_n, gain1, grad_hidden),
            moved=6 * MIB,
            name="last",
        )
        wide = (gown + gpair.astype(F32)).astype(BF)
        wide = lax.psum(wide, "expert").astype(F32)
        outputs = call(
            output_kernel,
            [((rows, D), BF)],
            (lengths, came_out, slots, hidden),
            [SM] + [VM] * 3,
            flops=2 * spots * rows * D,
            moved=8 * MIB,
            name="outputs",
        )[0]
        go_stay = came_go[0]

    if line:
        attn_sum, moe_sum = attn_sum.reshape(D), moe_sum.reshape(D)
        router_sum = jnp.transpose(router_sum)
    else:
        gwt, gow = wide[: 3 * inner], wide[3 * inner :]
        own_bias = gbias0[:heads, :NB].reshape(1, -1)
        pair_bias = gbias1[:heads, :NB].reshape(1, -1)
        ranks = jnp.arange(4, dtype=jnp.int32)[:, None]
        bias_parts = jnp.where(ranks == rank, own_bias, 0.0) + jnp.where(
            ranks == (rank ^ 2), pair_bias, 0.0
        )
        small = jnp.concatenate(
            [attn_part[0], moe_part[0], jnp.transpose(grad_router).reshape(-1), bias_parts.reshape(-1)]
        )
        small = lax.psum(small, ("expert", "tensor"))
        attn_sum, moe_sum = small[:D], small[D : 2 * D]
        router_sum = small[2 * D : 2 * D + experts * D].reshape(D, experts)
        bias_sum = lax.dynamic_slice(
            small[2 * D + experts * D :].reshape(4, heads * NB), (rank, 0), (1, heads * NB)
        )
    grad_weights = stay.astype(F32) + go_stay.astype(F32) + came_away.astype(F32)
    return (
        outputs,
        grad_inputs,
        attn_sum,
        jnp.transpose(gwt).reshape(D, 3, inner),
        gow,
        jnp.transpose(bias_sum.reshape(heads, NB)),
        moe_sum,
        router_sum,
        grad_weights[:D][None],
        jnp.transpose(grad_weights[D:])[None],
    )


def solution(mesh):
    return jax.shard_map(
        shards,
        mesh=mesh,
        in_specs=(
            P(("expert", "tensor"), None),
            P("expert"),
            P(("expert", "tensor"), None),
            P(),
            P(None, None, "tensor"),
            P("tensor", None),
            P(None, "tensor"),
            P(),
            P(),
            P("expert", None, "tensor"),
            P("expert", "tensor", None),
            P(("expert", "tensor"), None),
        ),
        out_specs=(
            P(("expert", "tensor"), None),
            P(("expert", "tensor"), None),
            P(),
            P(None, None, "tensor"),
            P("tensor", None),
            P(None, "tensor"),
            P(),
            P(),
            P("expert", None, "tensor"),
            P("expert", "tensor", None),
        ),
        check_vma=False,
    )
```

profile of v0, /device:TPU:8, one launch (start us, length us, event | category | flops | bytes accessed | tf_op | source)
XLA Modules:
  0.0 323.6 jit_solution(16421512485156468779)
XLA Ops:
  0.6 1.3 reshape.38.gain1_ref
  1.9 1.3 reshape.40.gain2_ref
  3.2 78.2 %begin.1 = (bf16[1024,768]{1,0:T(8,128)(2,1)}, bf16[576,1024]{1,0:T(8,128)(2,1)}, bf16[192,1024]{1,0:T(8,128)(2,1)}, f32[8,1024]{1,0:T(8,128)}, bf16[576,1024]{1...) custom-call(s32[2]{0:T(128)} %lengths_ref.3, ...), custom_call_target="tpu_custom_call" | custom-call | bytes 209715200 | tf_op jit(solution)/shard_map/begin/pallas_call | solution.py:1577
  81.4 107.5 %experts_line.1 = (bf16[2048,768]{1,0:T(8,128)(2,1)}, bf16[2048,768]{1,0:T(8,128)(2,1)}, bf16[1536,768]{1,0:T(8,128)(2,1)}, bf16[1536,768]{1,0:T(8,128)(2,1)}, b...) custom-call(bf16[512,768]{1,0:T(8,128)(2,1)} %get-tuple-element.45.normed_ref, f32[8,512]{1,0:T(8,128)} %get-tuple-element.46.info_in, ...), custom_call_target="tpu_custom_call" | custom-call | flops 57982058496 | bytes 62914560 | tf_op jit(solution)/shard_map/experts_line/pallas_call | solution.py:933
  188.9 117.9 %finish.1 = (bf16[512,768]{1,0:T(8,128)(2,1)}, bf16[512,768]{1,0:T(8,128)(2,1)}, f32[576,768]{1,0:T(8,128)}, f32[192,768]{1,0:T(8,128)}, f32[1,768]{1,0:T(1,128)...) custom-call(s32[2]{0:T(128)} %lengths_ref.3, ...), custom_call_target="tpu_custom_call" | custom-call | bytes 209715200 | tf_op jit(solution)/shard_map/finish/pallas_call | solution.py:1346
  306.8 1.3 reduce
  308.1 1.3 reduce.1
  309.3 3.9 %convert_add_fusion = f32[1536,768]{1,0:T(8,128)S(1)} fusion(bf16[1536,768]{1,0:T(8,128)(2,1)} %get-tuple-element.77, bf16[1536,768]{1,0:T(8,128)(2,1)} %get-tuple-element.76, bf16[1536,768]{1,0:T(8,128)(2,1)} %get-tuple-element.75), kind=kLoop, calls=%fused_computation | loop fusion | flops 5898240 | bytes 11796480 | tf_op jit(solution)/shard_map/add | solution.py:1795
  313.2 1.7 slice_bitcast_fusion
  314.9 0.0 copy-start.1
  314.9 1.9 copy.22
  316.9 0.0 copy-start
  316.9 2.2 copy.29
  319.1 0.0 copy-done.1
  319.1 0.0 copy-start.2
  319.1 0.9 copy.30
  319.9 0.0 copy-done
  319.9 1.2 copy.31
  321.2 0.0 copy-done.2
  321.2 0.8 copy.32
  322.0 0.0 copy-done.4
  322.0 0.6 copy.33
  322.6 0.0 copy-done.3
  322.6 0.6 copy.34
  (2 shorter events, 0.0 us)
Async XLA Ops:
  314.9 4.1 %copy-start.1 = (bf16[512,768]{1,0:T(8,128)(2,1)S(1)}, bf16[512,768]{1,0:T(8,128)(2,1)}, u32[]{:S(2)}) copy-start(bf16[512,768]{1,0:T(8,128)(2,1)} %get-tuple-element.101) | copy-start | bytes 2359300
  316.9 3.1 copy-start
  319.1 2.1 copy-start.2
  319.9 2.0 copy-start.4
  319.9 2.6 copy-start.3
where the time goes:
time: 330 us; the launch traced here: 324 us
  Pallas kernels  304 us (92%)
  local copies, waits for them, and re-layouts  12.5 us (4%)
  other arithmetic  6.43 us (2%)
    pallas_call x1, Pallas kernels, finish(): pl.pallas_call(functools.partial(finish_kernel, heads, cap), out_shape=[j...  118 us
    pallas_call x1, Pallas kernels, moe_line(): pl.pallas_call(functools.partial(expert_line_kernel, cap), out_shape=[jax...  108 us
    pallas_call x1, Pallas kernels, begin(): pl.pallas_call(functools.partial(begin_kernel, heads, cap), out_shape=[ja...  78.2 us
    unnamed x17, local copies, waits for them, and re-layouts  8.24 us

commit v1 on v0

--- a/solution.py
+++ b/solution.py
@@ -73,6 +73,10 @@
     return jnp.clip(own_length(lengths_ref) - half * rows, 0, rows)
 
 
+def as_row(ref):
+    return ref[...].reshape(1, D)
+
+
 VM = pl.BlockSpec(memory_space=pltpu.VMEM)
 SM = pl.BlockSpec(memory_space=pltpu.SMEM)
 
@@ -165,7 +169,7 @@
         for source, place in ((own_ref, core), (other_ref, 1 - core)):
             x = source[...].astype(F32)
             normed_ref[pl.ds(pl.multiple_of(place * half, half), half), :] = (
-                x * rms(x) * gain_ref[...]
+                x * rms(x) * as_row(gain_ref)
             ).astype(BF)
     else:
         normed_ref, w_ref, ow_ref, part_in = refs[:4]
@@ -203,7 +207,7 @@
         send_ref[...] = part_ref[pl.ds(pl.multiple_of((1 - core) * half, half), half), :].astype(BF)
 
 
-def attn_bwd_kernel(last, heads, lengths_ref, table_ref, *refs):
+def attn_bwd_kernel(early, last, heads, lengths_ref, table_ref, *refs):
     if last:
         (normed_ref, w_ref, ow_ref, qkvt_ref, mixt_ref, lse_ref, own_ref, other_ref, part_in) = refs[:9]
         gw_ref, gbias_ref, keep_ref, send_ref, ga_ref, got_ref, gt_ref, d0_ref, d1_ref, part_ref = refs[9:]
@@ -217,6 +221,8 @@
     ga_ref[pl.ds(pl.multiple_of((1 - core) * half, half), half), :] = other_ref[...]
     got_ref[...] = dot(ow_ref[...], ga_ref[...], 1, 1).astype(BF)
     gw_ref[3 * local_inner :] = dot(mixt_ref[...], ga_ref[...]).astype(gw_ref.dtype)
+    if early is not None:
+        early()
     masks = mask_block(own_length(lengths_ref))
     gbias_ref[...] = jnp.zeros_like(gbias_ref)
     ahead = iota((TILE, TILE), 1) >= iota((TILE, TILE), 0)
@@ -317,7 +323,7 @@
 def hidden_rows(x_ref, keep_ref, got_ref, gain_ref, hidden_ref):
     hidden = x_ref[...].astype(F32) + keep_ref[...] + got_ref[...].astype(F32)
     hidden_ref[...] = hidden
-    return (hidden * rms(hidden) * gain_ref[...]).astype(BF)
+    return (hidden * rms(hidden) * as_row(gain_ref)).astype(BF)
 
 
 def middle_kernel(
@@ -413,11 +419,13 @@
         store(step, step % 2, stay_ref).wait()
 
 
-def expert_rows(x, geo, here, w_ref, xt_ref, geot_ref, act_ref, gi_ref, acc_ref):
+def expert_rows(ready, x, geo, here, w_ref, xt_ref, geot_ref, act_ref, gi_ref, acc_ref):
     xt_ref[:, here] = x.T
     geot_ref[:, here] = geo.T
     worth = 0.0
-    for q in range(4):
+    for q in (0, 2, 1, 3):
+        if q == 1:
+            ready()
         inner = dot(x, w_ref[q, :D])
         grad_active = dot(geo, w_ref[q, D:], 1, 1)
         act, slope = gelu_pair(inner)
@@ -540,7 +548,7 @@
         gy = jnp.concatenate([grads_ref[rows_of(source(j * group + i)), :] for i in range(group)], axis=0)
         geo = (gate * gy.astype(F32)).astype(BF)
         x = x_ref[here, :]
-        worth = expert_rows(x, geo, here, w_ref, xt_ref, geot_ref, act_ref, gi_ref, acc_ref)
+        worth = expert_rows(lambda: None, x, geo, here, w_ref, xt_ref, geot_ref, act_ref, gi_ref, acc_ref)
         ids = iota((span, experts), 1)
         signs = (ids == me).astype(F32) - (ids + 1 == code).astype(F32)
         share = jnp.where(code > 0, (1.0 - gate) * worth, 0.0) * signs
@@ -679,7 +687,7 @@
         pltpu.make_async_copy(normed_ref, block_ref.at[place], local_sem.at[1]),
     )
     each(own, lambda c: c.start())
-    rest = D // 2
+    rest = D // 4 * 3
     far_down = tensor_copy(down_ref.at[rest:], w_ref.at[1, D + rest :], y_send, y_recv, away)
     far_down.start()
     grads_load = pltpu.make_async_copy(grads_in, grads_ref, grads_sem)
@@ -700,7 +708,7 @@
 
     weights = (
         (up_ref, 0, 0, D), (down_ref, 0, D, D), (far_up_ref, 1, 0, D), (far_half_ref, 1, D, rest),
-        (w_ref.at[1, D + rest :], 1, D + rest, rest),
+        (w_ref.at[1, D + rest :], 1, D + rest, D - rest),
     )
 
     def load(i):
@@ -756,9 +764,13 @@
         step = i + inward * (1 - i // 2 - 2 * (i // 2 - i // (LINE - 1)))
         return step + mirror * (LINE - 1 - 2 * step)
 
-    def chunk_at(c):
-        part = lax.rem(c + 1, 2) - (7 - c) // 7 + c // 7
-        return part, block_at((c + 1) // 2 - part * ((c + 1) // 2 - (c - 1) // 2))
+    outer = sum(d * 8**i for i, d in enumerate((0, 1, 4, 2, 5, 3, 6, 7)))
+    inner = sum(d * 8**i for i, d in enumerate((0, 1, 4, 2, 5, 3, 6, 7)))
+    chunks = outer + inward * (inner - outer)
+
+    def chunk_at(power):
+        digit = lax.rem(chunks // power, 8)
+        return digit // 4, block_at(lax.rem(digit, 4))
 
     for i in range(2):
 
@@ -767,21 +779,29 @@
             select(place + 2 * i - 1)
 
     grads_load.wait()
-    for i in range(4):
+    for i in range(2):
         load(i).wait()
         lend(i).wait_recv()
-    far_down.wait_recv()
-    lend(4).start()
-    lend(4).wait_recv()
-
-    def chunk(c, carry):
+
+    def far_ready(c):
+        @pl.when(c == 0)
+        def _():
+            far_down.wait_recv()
+            lend(4).start()
+            for i in (2, 3):
+                load(i).wait()
+                lend(i).wait_recv()
+            lend(4).wait_recv()
+
+
+    def chunk(c, power):
         for distance in range(2, LINE):
 
             @pl.when(c == 4 * distance - 7)
             def _():
                 line_accept(place, distance, along, select)
 
-        part, block = chunk_at(c)
+        part, block = chunk_at(power)
 
         @pl.when(part == 1)
         def _():
@@ -793,7 +813,7 @@
         code = meta[:, 3:4].astype(jnp.int32)
         geo = (gate * grads_ref[part, block].astype(F32)).astype(BF)
         x = x_ref[part, block]
-        worth = expert_rows(x, geo, here, w_ref, xt_ref, geot_ref, act_ref, gi_ref, acc_ref)
+        worth = expert_rows(lambda: far_ready(c), x, geo, here, w_ref, xt_ref, geot_ref, act_ref, gi_ref, acc_ref)
         ids = iota((cap, experts), 1)
         signs = (ids == me).astype(F32) - (ids + 1 == code).astype(F32)
         share = jnp.where(code > 0, (1.0 - gate) * worth, 0.0) * signs
@@ -806,9 +826,9 @@
         def _():
             give_back(part, block).start()
 
-        return carry
-
-    lax.fori_loop(0, count, chunk, 0)
+        return power * 8
+
+    lax.fori_loop(0, count, chunk, jnp.int32(1))
     own_back = pltpu.make_async_copy(x_ref.at[0, place], came_ref.at[rows_of(me)], local_sem.at[0])
     own_back.start()
 
@@ -816,7 +836,7 @@
         first = step // (D // TILE) * LINE
         cols, total = expert_outs(first * cap, LINE * cap, lax.rem(step, D // TILE), act_ref, w_ref)
         for i in range(LINE):
-            part, block = chunk_at(first + i)
+            part, block = chunk_at((1 + first // LINE * (8**LINE - 1)) * 8**i)
             meta = meta_ref[part, block].T
             gate = meta[:, 0:1] + meta[:, 1:2] + meta[:, 2:3]
             result_ref[rows_of(origin(part, block)), cols] = (
@@ -854,7 +874,7 @@
     scale = rms(hidden)
     unit = hidden * scale
     gain_out[...] = jnp.broadcast_to(jnp.sum(gn * unit, axis=0, keepdims=True), gain_out.shape)
-    g = gn * gain_ref[...]
+    g = gn * as_row(gain_ref)
     valid = (iota((hidden.shape[0], 1), 0) < own_valid(lengths_ref, hidden.shape[0])).astype(F32)
     gh = scale * (g - unit * jnp.mean(g * unit, axis=1, keepdims=True)) + valid * grad_ref[...].astype(F32)
     gh_ref[...] = gh
@@ -874,7 +894,7 @@
     unit = x * scale
     gn = keep_ref[...] + got_ref[...].astype(F32)
     gain_out[...] = jnp.broadcast_to(jnp.sum(gn * unit, axis=0, keepdims=True), gain_out.shape)
-    g = gn * gain_ref[...]
+    g = gn * as_row(gain_ref)
     out_ref[...] = (
         gh_ref[...] + scale * (g - unit * jnp.mean(g * unit, axis=1, keepdims=True))
     ).astype(BF)
@@ -1051,7 +1071,7 @@
     unit = x * scale
     gn = keep_ref[...] + got_ref[...].astype(F32)
     attn = jnp.sum(gn * unit, axis=0, keepdims=True)
-    g = gn * gain_ref[...]
+    g = gn * as_row(gain_ref)
     gin_out[...] = (gh_ref[...] + scale * (g - unit * jnp.mean(g * unit, axis=1, keepdims=True))).astype(BF)
 
     heads = gow_out.shape[0] // HD
@@ -1163,8 +1183,8 @@
             d_recv.at[number],
             mate,
         ).wait_recv()
-    attn_out[...] = jnp.concatenate([small_out[6, i : i + 1] for i in range(6)], axis=1)
-    moe_out[...] = jnp.concatenate([small_out[7, i : i + 1] for i in range(6)], axis=1)
+    attn_out[...] = jnp.concatenate([small_out[6, i : i + 1] for i in range(6)], axis=1).reshape(D)
+    moe_out[...] = jnp.concatenate([small_out[7, i : i + 1] for i in range(6)], axis=1).reshape(D)
     router_out[...] = jnp.concatenate([small_out[j] for j in range(D // 128)], axis=1)
     bias = functools.reduce(
         jnp.add,
@@ -1194,10 +1214,10 @@
 
 def finish_kernel(
     heads, cap, lengths_ref,
-    table0_ref, table1_ref, came_ref, slots_ref, hidden_ref, gain2_ref, grad_ref, gain1_ref, router_ref,
-    result_in, go_in, away_in, x_in, normed_in, wt_in, ow_in, pw_in, qkvt0_in, mixt0_in, lse0_in, qkvt1_in, mixt1_in, lse1_in,
+    table0_ref, table1_ref, slots_ref, gain2_ref, gain1_ref, router_ref,
+    came_in, hidden_in, grad_in, result_in, go_in, away_in, x_in, normed_in, wt_in, ow_in, pw_in, qkvt0_in, mixt0_in, lse0_in, qkvt1_in, mixt1_in, lse1_in,
     out_ref, gin_out, gwt_out, gow_out, attn_out, moe_out, router_out, bias_out, came_go_ref, came_away_ref,
-    outs_ref, gorecv_ref, away_ref, x_ref, normed_ref, wt_ref, ow_ref, pw_ref, qkvt0_ref, mixt0_ref, lse0_ref, qkvt1_ref, mixt1_ref, lse1_ref,
+    came_ref, hidden_ref, grad_ref, outs_ref, gorecv_ref, away_ref, x_ref, normed_ref, wt_ref, ow_ref, pw_ref, qkvt0_ref, mixt0_ref, lse0_ref, qkvt1_ref, mixt1_ref, lse1_ref,
     gh_ref, ga_ref, other_ref, moe_ref, gpart_ref, gpair_ref, gown_ref, bias0_ref, bias1_ref, keep_ref, send_ref,
     all_ga_ref, got_ref, gt_ref, d0_ref, d1_ref, npart_ref,
     o_send, o_recv, v_send, v_recv, y_send, y_recv, w_send, w_recv, e_send, e_recv, load_sem, *tail_refs,
@@ -1207,40 +1227,10 @@
     rank = lax.axis_index("tensor")
     core = flipped(rank, 1, 4)
     away_rank = flipped(rank, 2, 4)
-    barrier = pltpu.get_barrier_semaphore()
-    for k in range(1, count):
-        pl.semaphore_signal(
-            barrier, inc=1, device_id={"expert": flipped(me, k, count)}, device_id_type=pl.DeviceIdType.MESH
-        )
-    for k in range(1, 4):
-        pl.semaphore_signal(
-            barrier, inc=1, device_id={"tensor": flipped(rank, k, 4)}, device_id_type=pl.DeviceIdType.MESH
-        )
-    pl.semaphore_wait(barrier, count + 2)
-
-    def rows_of(number):
-        return pl.ds(pl.multiple_of(number * cap, cap), cap)
-
-    def result(k):
-        return mesh_copy(
-            result_in.at[rows_of(flipped(me, k, count))],
-            outs_ref.at[rows_of(me)],
-            o_send.at[k],
-            o_recv.at[k],
-            flipped(me, k, count),
-        )
-
-    order = list(range(LINE, count)) + list(range(1, LINE))
-    for k in order:
-        result(k).start()
-    own_result = pltpu.make_async_copy(result_in.at[rows_of(me)], outs_ref.at[rows_of(me)], load_sem.at[0])
-    own_result.start()
-    away_load = pltpu.make_async_copy(away_in, away_ref, load_sem.at[1])
-    away_load.start()
-    go_away = tensor_copy(go_in.at[1], gorecv_ref, v_send.at[0], v_recv.at[0], core)
-    go_away.start()
-    go_stay = tensor_copy(go_in.at[0], came_go_ref, v_send.at[1], v_recv.at[1], core)
     places = (
+        (came_in, came_ref),
+        (hidden_in, hidden_ref),
+        (grad_in, grad_ref),
         (normed_in, normed_ref),
         (pw_in, pw_ref),
         (qkvt1_in, qkvt1_ref),
@@ -1256,7 +1246,41 @@
     loads = [pltpu.make_async_copy(a, b, load_sem.at[i + 2]) for i, (a, b) in enumerate(places)]
     for load in loads:
         load.start()
-
+    barrier = pltpu.get_barrier_semaphore()
+    for k in range(1, count):
+        pl.semaphore_signal(
+            barrier, inc=1, device_id={"expert": flipped(me, k, count)}, device_id_type=pl.DeviceIdType.MESH
+        )
+    for k in range(1, 4):
+        pl.semaphore_signal(
+            barrier, inc=1, device_id={"tensor": flipped(rank, k, 4)}, device_id_type=pl.DeviceIdType.MESH
+        )
+    pl.semaphore_wait(barrier, count + 2)
+
+    def rows_of(number):
+        return pl.ds(pl.multiple_of(number * cap, cap), cap)
+
+    def result(k):
+        return mesh_copy(
+            result_in.at[rows_of(flipped(me, k, count))],
+            outs_ref.at[rows_of(me)],
+            o_send.at[k],
+            o_recv.at[k],
+            flipped(me, k, count),
+        )
+
+    order = list(range(LINE, count)) + list(range(1, LINE))
+    for k in order:
+        result(k).start()
+    own_result = pltpu.make_async_copy(result_in.at[rows_of(me)], outs_ref.at[rows_of(me)], load_sem.at[0])
+    own_result.start()
+    away_load = pltpu.make_async_copy(away_in, away_ref, load_sem.at[1])
+    away_load.start()
+    go_away = tensor_copy(go_in.at[1], gorecv_ref, v_send.at[0], v_recv.at[0], core)
+    go_away.start()
+    go_stay = tensor_copy(go_in.at[0], came_go_ref, v_send.at[1], v_recv.at[1], core)
+    for load in loads[:3]:
+        load.wait()
     turn_kernel(lengths_ref, came_ref, slots_ref, hidden_ref, gain2_ref, grad_ref, gh_ref, ga_ref, moe_ref)
     ga_swap = tensor_copy(ga_ref, other_ref, w_send, w_recv, core)
     ga_swap.start()
@@ -1276,29 +1300,34 @@
         away_ref[lines(i)] = (
             away_ref[lines(i)].astype(F32) + gorecv_ref[lines(i)].astype(F32)
         ).astype(BF)
-        if i < 2:
+        if i < 1:
             away(i).start()
     ga_swap.wait()
     go_stay.start()
-    for load in loads:
+    for load in loads[3:]:
         load.wait()
     inner = heads * HD
+    split = ((slice(3 * inner, 4 * inner), 0), (slice(0, 3 * inner), 1))
+    pair = [
+        tensor_copy(gpart_ref.at[lines_of], gpair_ref.at[lines_of], e_send.at[i], e_recv.at[i], away_rank)
+        for lines_of, i in split
+    ]
     attn_bwd_kernel(
-        False, heads, lengths_ref, table1_ref,
+        pair[0].start, False, heads, lengths_ref, table1_ref,
         normed_ref, pw_ref.at[: 3 * inner], pw_ref.at[3 * inner :], qkvt1_ref, mixt1_ref, lse1_ref, ga_ref, other_ref,
         gpart_ref, bias1_ref, npart_ref, all_ga_ref, got_ref, gt_ref, d0_ref, d1_ref,
     )
-    pair = tensor_copy(gpart_ref, gpair_ref, e_send, e_recv, away_rank)
-    pair.start()
+    pair[1].start()
     attn_bwd_kernel(
-        True, heads, lengths_ref, table0_ref,
+        None, True, heads, lengths_ref, table0_ref,
         normed_ref, wt_ref, ow_ref, qkvt0_ref, mixt0_ref, lse0_ref, ga_ref, other_ref, npart_ref,
         gown_ref, bias0_ref, keep_ref, send_ref, all_ga_ref, got_ref, gt_ref, d0_ref, d1_ref, npart_ref,
     )
 
     def pair_done():
-        pair.wait_recv()
-        for i in range(2, PARTS):
+        for one in pair:
+            one.wait_recv()
+        for i in range(1, PARTS):
             away(i).start()
 
     def beside():
@@ -1313,7 +1342,8 @@
     )
     for k in order:
         result(k).wait_send()
-    pair.wait_send()
+    for one in pair:
+        one.wait_send()
     go_away.wait_send()
     go_stay.wait()
     for i in range(PARTS):
@@ -1324,13 +1354,14 @@
     dma = pltpu.SemaphoreType.DMA
     count = 2 * LINE
     spots = count * cap
-    rows = arrays[4].shape[0]
+    rows = others[1].shape[0]
     local = heads * HD
     part = 4 * local // count
     anyspec = pl.BlockSpec(memory_space=pl.ANY)
     half = (rows, D)
     tail_sems = [dma((LINE,))] * 8 + [dma, dma] + [dma((count,))] * 2 + [dma((4,))] * 2 + [dma((count,))] * 2
     shapes = [
+        ((spots, D), BF), (half, F32), (half, BF),
         ((spots, D), BF), ((2 * D, D), BF), ((2 * D, D), BF), (half, BF), ((SEQ, D), BF), ((3 * local, D), BF),
         ((local, D), BF), ((4 * local, D), BF), ((3 * local, SEQ), BF), ((local, SEQ), BF), ((8, SEQ), F32),
         ((3 * local, SEQ), BF), ((local, SEQ), BF), ((8, SEQ), F32),
@@ -1350,8 +1381,8 @@
             jax.ShapeDtypeStruct(half, BF),
             jax.ShapeDtypeStruct((3 * local, D), F32),
             jax.ShapeDtypeStruct((local, D), F32),
-            jax.ShapeDtypeStruct((1, D), F32),
-            jax.ShapeDtypeStruct((1, D), F32),
+            jax.ShapeDtypeStruct((D,), F32),
+            jax.ShapeDtypeStruct((D,), F32),
             jax.ShapeDtypeStruct((count, D), F32),
             jax.ShapeDtypeStruct((heads, NB), F32),
             jax.ShapeDtypeStruct((2 * D, D), BF),
@@ -1360,7 +1391,7 @@
         in_specs=[SM] * len(scalars) + [VM] * len(arrays) + [anyspec] * len(others),
         out_specs=[VM] * 8 + [anyspec] * 2,
         scratch_shapes=[pltpu.VMEM(*v) for v in shapes]
-        + [dma((count,)), dma((count,)), dma((2,)), dma((2,)), dma((PARTS,)), dma((PARTS,)), dma, dma, dma, dma, dma((16,))]
+        + [dma((count,)), dma((count,)), dma((2,)), dma((2,)), dma((PARTS,)), dma((PARTS,)), dma, dma, dma((2,)), dma((2,)), dma((16,))]
         + [pltpu.VMEM(*v) for v in tail_shapes]
         + tail_sems,
         compiler_params=pltpu.CompilerParams(
@@ -1444,7 +1475,7 @@
         one.start()
     far = (
         tensor_copy(up_ref, far_up_ref, y_send.at[3], y_recv.at[3], away),
-        tensor_copy(down_ref.at[: D // 2], far_half_ref, y_send.at[4], y_recv.at[4], away),
+        tensor_copy(down_ref.at[: D // 4 * 3], far_half_ref, y_send.at[4], y_recv.at[4], away),
     )
 
     def along(block, step):
@@ -1568,7 +1599,7 @@
     ]
     outs = kept + [
         (half, F32), (half, BF), ((8, rows), F32), ((8, rows), F32), ((4 * local, D), BF), ((heads, NB), F32),
-        ((2, LINE, cap, D), BF), ((D, D), BF), ((D // 2, D), BF), ((2, rows, D), BF), ((2, 8, rows), F32),
+        ((2, LINE, cap, D), BF), ((D, D), BF), ((D // 4 * 3, D), BF), ((2, rows, D), BF), ((2, 8, rows), F32),
     ]
     shapes = [
         (half, BF), (half, BF), ((SEQ, D), F32), (half, F32), (half, BF), ((LINE, rows, D), BF), ((LINE, 8, rows), F32),
@@ -1617,8 +1648,7 @@
     def swap(x, bit):
         return lax.ppermute(x, "tensor", [(i, i ^ bit) for i in range(4)])
 
-    gain1 = attn_gain.reshape(1, D)
-    gain2 = moe_gain.reshape(1, D)
+    gain1, gain2 = attn_gain, moe_gain
     wt = jnp.transpose(qkv_weight.reshape(D, 3 * inner))
     routes_t = jnp.transpose(routes)
     up, down = up_weight[0], down_weight[0]
@@ -1703,8 +1733,8 @@
             heads,
             cap,
             (lengths,),
-            (table, pair_table, came, slots, hidden, gain2, out_grad, gain1, grad_router),
-            (result, go, away, inputs, normed, wt, out_weight, pair_w, qkvt0, mixt0, lse0, qkvt1, mixt1, lse1),
+            (table, pair_table, slots, gain2, gain1, grad_router),
+            (came, hidden, out_grad, result, go, away, inputs, normed, wt, out_weight, pair_w, qkvt0, mixt0, lse0, qkvt1, mixt1, lse1),
         )
     else:
         came_out = exchange(result)
@@ -1731,7 +1761,7 @@
             pltpu.VMEM((TILE, TILE), F32),
         ]
         gpart, gbias1, npart = call(
-            functools.partial(attn_bwd_kernel, False, heads),
+            functools.partial(attn_bwd_kernel, None, False, heads),
             [((4 * inner, D), BF), ((8, 128), F32), ((SEQ, D), F32)],
             (lengths, pair_table, normed, wt1, ow1, qkvt1, mixt1, lse1, grad_attended, other_grad),
             [SM] + [VM] * 1 + [VM] * 8,
@@ -1741,7 +1771,7 @@
         )
         gpair = swap(gpart, 2)
         gown, gbias0, keep_n, send_n = call(
-            functools.partial(attn_bwd_kernel, True, heads),
+            functools.partial(attn_bwd_kernel, None, True, heads),
             [((4 * inner, D), F32), ((8, 128), F32), ((rows, D), F32), ((rows, D), BF)],
             (lengths, table, normed, wt, out_weight, qkvt0, mixt0, lse0, grad_attended, other_grad, npart),
             [SM] + [VM] * 1 + [VM] * 9,
@@ -1773,7 +1803,6 @@
         go_stay = came_go[0]
 
     if line:
-        attn_sum, moe_sum = attn_sum.reshape(D), moe_sum.reshape(D)
         router_sum = jnp.transpose(router_sum)
     else:
         gwt, gow = wide[: 3 * inner], wide[3 * inner :]
@@ -1792,7 +1821,10 @@
         bias_sum = lax.dynamic_slice(
             small[2 * D + experts * D :].reshape(4, heads * NB), (rank, 0), (1, heads * NB)
         )
-    grad_weights = stay.astype(F32) + go_stay.astype(F32) + came_away.astype(F32)
+    grad_up, grad_down = (
+        stay[rows_of].astype(F32) + go_stay[rows_of].astype(F32) + came_away[rows_of].astype(F32)
+        for rows_of in (slice(0, D), slice(D, 2 * D))
+    )
     return (
         outputs,
         grad_inputs,
@@ -1802,8 +1834,8 @@
         jnp.transpose(bias_sum.reshape(heads, NB)),
         moe_sum,
         router_sum,
-        grad_weights[:D][None],
-        jnp.transpose(grad_weights[D:])[None],
+        grad_up[None],
+        jnp.transpose(grad_down)[None],
     )
 
 

time: 330 us -> 317 us (0.961)
  the two profiles are of different devices: /device:TPU:8 before, /device:TPU:14 now
where the time goes in v1:
time: 317 us; the launch traced here: 311 us
  Pallas kernels  295 us (93%)
  local copies, waits for them, and re-layouts  9.44 us (3%)
  other arithmetic  5.21 us (2%)
    pallas_call x1, Pallas kernels, finish(): pl.pallas_call(functools.partial(finish_kernel, heads, cap), out_shape=[j...  115 us
    pallas_call x1, Pallas kernels, moe_line(): pl.pallas_call(functools.partial(expert_line_kernel, cap), out_shape=[jax...  101 us
    pallas_call x1, Pallas kernels, begin(): pl.pallas_call(functools.partial(begin_kernel, heads, cap), out_shape=[ja...  79.2 us
    unnamed x23, local copies, waits for them, and re-layouts  9.44 us

profile of v1, /device:TPU:14, one launch (start us, length us, event | category | flops | bytes accessed | tf_op | source)
XLA Modules:
  0.0 311.1 jit_solution(18363526978859545337)
XLA Ops:
  0.6 79.2 %begin.1 = (bf16[1024,768]{1,0:T(8,128)(2,1)}, bf16[576,1024]{1,0:T(8,128)(2,1)}, bf16[192,1024]{1,0:T(8,128)(2,1)}, f32[8,1024]{1,0:T(8,128)}, bf16[576,1024]{1...) custom-call(s32[2]{0:T(128)} %lengths_ref.3, ...), custom_call_target="tpu_custom_call" | custom-call | bytes 209715200 | tf_op jit(solution)/shard_map/begin/pallas_call | solution.py:1608
  79.8 101.1 %experts_line.1 = (bf16[2048,768]{1,0:T(8,128)(2,1)}, bf16[2048,768]{1,0:T(8,128)(2,1)}, bf16[1536,768]{1,0:T(8,128)(2,1)}, bf16[1536,768]{1,0:T(8,128)(2,1)}, b...) custom-call(bf16[512,768]{1,0:T(8,128)(2,1)} %get-tuple-element.46.normed_ref, f32[8,512]{1,0:T(8,128)} %get-tuple-element.47.info_in, ...), custom_call_target="tpu_custom_call" | custom-call | flops 57982058496 | bytes 62914560 | tf_op jit(solution)/shard_map/experts_line/pallas_call | solution.py:953
  180.9 115.1 %finish.1 = (bf16[512,768]{1,0:T(8,128)(2,1)}, bf16[512,768]{1,0:T(8,128)(2,1)}, f32[576,768]{1,0:T(8,128)}, f32[192,768]{1,0:T(8,128)}, f32[768]{0:T(1024)}, /*...) custom-call(s32[2]{0:T(128)} %lengths_ref.3, ...), custom_call_target="tpu_custom_call" | custom-call | bytes 209715200 | tf_op jit(solution)/shard_map/finish/pallas_call | solution.py:1377
  296.0 5.2 %add_bitcast_fusion = (f32[1,768,768]{1,2,0:T(8,128)S(1)}, f32[1,768,768]{2,1,0:T(8,128)}) fusion(bf16[1536,768]{1,0:T(8,128)(2,1)} %get-tuple-element.77, bf16[1536,768]{1,0:T(8,128)(2,1)} %get-tuple-element.76, bf16[1536,768]{1,0:T(8,128)(2,1)} %get-tuple-element.75), kind=kLoop, calls=%fused_computation | loop fusion | flops 5898240 | bytes 11796480 | tf_op jit(solution)/shard_map/broadcast_in_dim | solution.py:1838
  301.2 0.0 copy-start.1
  301.2 1.9 copy.22
  303.1 0.0 copy-start.5
  303.1 0.0 copy-start
  303.1 2.2 copy.31
  305.3 0.0 copy-done.1
  305.3 0.0 copy-start.2
  305.3 0.9 copy.32
  306.2 0.0 copy-done.5
  306.2 0.6 copy.33
  306.8 0.0 copy-done
  306.8 1.2 copy.34
  308.0 0.0 copy-done.2
  308.0 0.8 copy.35
  308.9 0.0 copy-done.6
  308.9 0.6 copy.36
  309.4 0.0 copy-done.4
  309.4 0.6 copy.37
  310.0 0.0 copy-done.3
  310.0 0.6 copy.38
  (3 shorter events, 0.0 us)
Async XLA Ops:
  301.2 4.1 %copy-start.1 = (bf16[512,768]{1,0:T(8,128)(2,1)S(1)}, bf16[512,768]{1,0:T(8,128)(2,1)}, u32[]{:S(2)}) copy-start(bf16[512,768]{1,0:T(8,128)(2,1)} %get-tuple-element.101) | copy-start | bytes 2359300
  303.1 3.1 copy-start.5
  303.1 3.7 %copy-start = (f32[576,768]{1,0:T(8,128)S(1)}, f32[576,768]{1,0:T(8,128)}, u32[]{:S(2)}) copy-start(f32[576,768]{1,0:T(8,128)} %get-tuple-element.70) | copy-start | bytes 5308420
  305.3 2.7 copy-start.2
  306.8 2.0 copy-start.6
  306.8 2.6 copy-start.4
  306.8 3.2 %copy-start.3 = (f32[8,768]{1,0:T(8,128)S(1)}, f32[8,768]{1,0:T(8,128)}, u32[]{:S(2)}) copy-start(f32[8,768]{1,0:T(8,128)} %get-tuple-element.74) | copy-start | bytes 73732

commit v2 on v1

--- a/solution.py
+++ b/solution.py
@@ -374,29 +374,29 @@
     return total
 
 
-def weight_grads(xt_ref, geot_ref, act_ref, gi_ref, stage_ref, stay_ref, away_ref, go_ref, out_sem):
+def weight_grads(xt_ref, geot_ref, act_ref, gi_ref, stage_ref, turned_ref, stay_ref, away_ref, go_ref, out_sem):
     tiles = D // TILE
     steps = 8 * tiles
 
     def columns(step):
         return pl.ds(pl.multiple_of(lax.rem(step, tiles) * TILE, TILE), TILE)
 
-    def store(step, slot, out_ref):
-        half = lax.rem(step, 2 * tiles) // tiles
-        return pltpu.make_async_copy(
-            stage_ref.at[slot],
-            out_ref.at[pl.ds(pl.multiple_of(half * D, D), D), columns(step)],
-            out_sem.at[slot],
-        )
+    def store(step, slot, out_ref, half):
+        if half:
+            there = pl.ds(pl.multiple_of(D + lax.rem(step, tiles) * TILE, TILE), TILE)
+            return pltpu.make_async_copy(turned_ref.at[slot], out_ref.at[there], out_sem.at[slot])
+        return pltpu.make_async_copy(stage_ref.at[slot], out_ref.at[:D, columns(step)], out_sem.at[slot])
 
     def weights(step, carry):
         q = step // (2 * tiles)
         half = lax.rem(step, 2 * tiles) // tiles
         slot = lax.rem(step, 2)
 
+        outs = (stay_ref, away_ref, go_ref.at[0], go_ref.at[1])
+
         @pl.when(step >= 2)
         def _():
-            store(step - 2, slot, stay_ref).wait()
+            store(step - 2, slot, stay_ref, 0).wait()
 
         @pl.when(half == 0)
         def _():
@@ -404,19 +404,20 @@
 
         @pl.when(half == 1)
         def _():
-            stage_ref[slot] = dot(geot_ref[...], act_ref[q, :, columns(step)]).astype(BF)
-
-        for number, out_ref in enumerate((stay_ref, away_ref, go_ref.at[0], go_ref.at[1])):
-
-            @pl.when(q == number)
-            def _():
-                store(step, slot, out_ref).start()
+            turned_ref[slot] = dot(geot_ref[...], act_ref[q, :, columns(step)]).astype(BF).T
+
+        for number, out_ref in enumerate(outs):
+            for kind in range(2):
+
+                @pl.when((q == number) & (half == kind))
+                def _():
+                    store(step, slot, out_ref, kind).start()
 
         return carry
 
     lax.fori_loop(0, steps, weights, 0)
     for step in (steps - 2, steps - 1):
-        store(step, step % 2, stay_ref).wait()
+        store(step, step % 2, stay_ref, 1).wait()
 
 
 def expert_rows(ready, x, geo, here, w_ref, xt_ref, geot_ref, act_ref, gi_ref, acc_ref):
@@ -454,7 +455,7 @@
 def expert_kernel(
     count, cap, packed_ref, send_meta_ref, grads_ref, router_ref, w0, w1, w2, w3,
     came_ref, result_ref, stay_ref, away_ref, go_ref, grouter_ref,
-    w_ref, x_ref, xt_ref, geot_ref, act_ref, gi_ref, gsend_ref, meta_ref, acc_ref, stage_ref,
+    w_ref, x_ref, xt_ref, geot_ref, act_ref, gi_ref, gsend_ref, meta_ref, acc_ref, stage_ref, turned_ref,
     x_send, x_recv, m_send, m_recv, r_send, r_recv, local_sem, w_sem, out_sem,
 ):
     me = lax.axis_index("expert")
@@ -580,7 +581,7 @@
         return carry
 
     lax.fori_loop(0, count // group * (D // TILE), results, 0)
-    weight_grads(xt_ref, geot_ref, act_ref, gi_ref, stage_ref, stay_ref, away_ref, go_ref, out_sem)
+    weight_grads(xt_ref, geot_ref, act_ref, gi_ref, stage_ref, turned_ref, stay_ref, away_ref, go_ref, out_sem)
     own_back.wait()
 
     def finish(k, carry):
@@ -608,8 +609,8 @@
 
 def expert_line_kernel(
     cap, normed_ref, info_in, router_ref, grads_in, near_ref, near_info_ref, up_ref, down_ref, far_up_ref, far_half_ref,
-    came_ref, result_ref, stay_ref, away_ref, go_ref, grouter_ref,
-    grads_ref, w_ref, block_ref, info_ref, x_ref, xs_ref, meta_ref, ms_ref, xt_ref, geot_ref, act_ref, gi_ref, acc_ref, stage_ref,
+    came_ref, result_out, stay_ref, away_ref, go_ref, grouter_ref,
+    result_ref, grads_ref, w_ref, block_ref, info_ref, x_ref, xs_ref, meta_ref, ms_ref, xt_ref, geot_ref, act_ref, gi_ref, acc_ref, stage_ref, turned_ref,
     b_send, b_recv, i_send, i_recv, x_send, x_recv, m_send, m_recv, r_send, r_recv, local_sem, w_sem, v_send, v_recv, y_send, y_recv, grads_sem, near_sem, out_sem,
 ):
     count = 2 * LINE
@@ -845,8 +846,11 @@
         return carry
 
     lax.fori_loop(0, 2 * (D // TILE), results, 0)
-    weight_grads(xt_ref, geot_ref, act_ref, gi_ref, stage_ref, stay_ref, away_ref, go_ref, out_sem)
+    leave = pltpu.make_async_copy(result_ref, result_out, local_sem.at[1])
+    leave.start()
+    weight_grads(xt_ref, geot_ref, act_ref, gi_ref, stage_ref, turned_ref, stay_ref, away_ref, go_ref, out_sem)
     own_back.wait()
+    leave.wait()
     for i in range(5):
         lend(i).wait_send()
     far_down.wait_send()
@@ -927,6 +931,7 @@
             pltpu.VMEM((experts, 8, cap), F32),
             pltpu.VMEM((CHUNK, D), F32),
             pltpu.VMEM((2, D, TILE), BF),
+            pltpu.VMEM((2, TILE, D), BF),
             dma((experts,)),
             dma((experts,)),
             dma((experts,)),
@@ -961,8 +966,9 @@
             jax.ShapeDtypeStruct((experts, D), F32),
         ],
         in_specs=[VM, VM, VM] + [anyspec] * 7,
-        out_specs=[anyspec, VM, anyspec, anyspec, anyspec, VM],
+        out_specs=[anyspec, anyspec, anyspec, anyspec, anyspec, VM],
         scratch_shapes=[
+            pltpu.VMEM((spots, D), BF),
             pltpu.VMEM((2, LINE, cap, D), BF),
             pltpu.VMEM((4, 2 * D, D), BF),
             pltpu.VMEM((LINE, rows, D), BF),
@@ -977,6 +983,7 @@
             pltpu.VMEM((4, spots, D), BF),
             pltpu.VMEM((cap, D), F32),
             pltpu.VMEM((2, D, TILE), BF),
+            pltpu.VMEM((2, TILE, D), BF),
             dma((2, LINE)),
             dma((LINE,)),
             dma((2, LINE)),
@@ -1559,6 +1566,7 @@
             mesh_copy(normed2_ref, near_ref.at[i], n_send.at[i + 2], n_recv.at[i + 2], target),
         )
 
+    line_sent(place, along, 0)
     for i in range(2):
 
         @pl.when(inside[1 - i])
@@ -1570,7 +1578,6 @@
     for block in range(LINE):
         keep(block).wait()
         across(block).wait()
-    line_sent(place, along, 0)
     for store in stores:
         store.wait()
     for one in pair:
@@ -1835,7 +1842,7 @@
         moe_sum,
         router_sum,
         grad_up[None],
-        jnp.transpose(grad_down)[None],
+        grad_down[None],
     )
 
 

time: 317 us -> 314 us (level)
  local copies, waits for them, and re-layouts: 9.44 us -> 6.19 us
    unnamed x23 -> x24, local copies, waits for them, and re-layouts: 9.44 us -> 6.19 us
where the time goes in v2:
time: 314 us; the launch traced here: 308 us
  Pallas kernels  294 us (94%)
  local copies, waits for them, and re-layouts  6.19 us (2%)
  other arithmetic  6.09 us (2%)
    pallas_call x1, Pallas kernels, finish(): pl.pallas_call(functools.partial(finish_kernel, heads, cap), out_shape=[j...  115 us
    pallas_call x1, Pallas kernels, moe_line(): pl.pallas_call(functools.partial(expert_line_kernel, cap), out_shape=[jax...  99.9 us
    pallas_call x1, Pallas kernels, begin(): pl.pallas_call(functools.partial(begin_kernel, heads, cap), out_shape=[ja...  79.2 us

profile of v2, /device:TPU:14, one launch (start us, length us, event | category | flops | bytes accessed | tf_op | source)
XLA Modules:
  0.0 307.6 jit_solution(1288880028696499897)
XLA Ops:
  0.6 79.2 %begin.1 = (bf16[1024,768]{1,0:T(8,128)(2,1)}, bf16[576,1024]{1,0:T(8,128)(2,1)}, bf16[192,1024]{1,0:T(8,128)(2,1)}, f32[8,1024]{1,0:T(8,128)}, bf16[576,1024]{1...) custom-call(s32[2]{0:T(128)} %lengths_ref.3, ...), custom_call_target="tpu_custom_call" | custom-call | bytes 209715200 | tf_op jit(solution)/shard_map/begin/pallas_call | solution.py:1615
  79.8 99.9 %experts_line.1 = (bf16[2048,768]{1,0:T(8,128)(2,1)}, bf16[2048,768]{1,0:T(8,128)(2,1)}, bf16[1536,768]{1,0:T(8,128)(2,1)}, bf16[1536,768]{1,0:T(8,128)(2,1)}, b...) custom-call(bf16[512,768]{1,0:T(8,128)(2,1)} %get-tuple-element.46.normed_ref, f32[8,512]{1,0:T(8,128)} %get-tuple-element.47.info_in, ...), custom_call_target="tpu_custom_call" | custom-call | flops 57982058496 | bytes 62914560 | tf_op jit(solution)/shard_map/experts_line/pallas_call | solution.py:958
  179.8 115.1 %finish.1 = (bf16[512,768]{1,0:T(8,128)(2,1)}, bf16[512,768]{1,0:T(8,128)(2,1)}, f32[576,768]{1,0:T(8,128)}, f32[192,768]{1,0:T(8,128)}, f32[768]{0:T(1024)}, /*...) custom-call(s32[2]{0:T(128)} %lengths_ref.3, ...), custom_call_target="tpu_custom_call" | custom-call | bytes 209715200 | tf_op jit(solution)/shard_map/finish/pallas_call | solution.py:1384
  294.8 0.0 copy-start.2
  294.8 0.0 copy-start.1
  294.8 6.1 %add_bitcast_fusion = (f32[1,768,768]{2,1,0:T(8,128)}, f32[1,768,768]{2,1,0:T(8,128)}) fusion(bf16[1536,768]{1,0:T(8,128)(2,1)} %get-tuple-element.77, bf16[1536,768]{1,0:T(8,128)(2,1)} %get-tuple-element.76, bf16[1536,768]{1,0:T(8,128)(2,1)} %get-tuple-element.75), kind=kLoop, calls=%fused_computation | loop fusion | flops 5898240 | bytes 11796480 | tf_op jit(solution)/shard_map/broadcast_in_dim | solution.py:1845
  300.9 0.0 copy-start.6
  300.9 0.0 copy-start
  300.9 0.0 copy-done.2
  301.0 0.9 copy.30
  301.8 0.0 copy-done.1
  301.8 0.9 copy.31
  302.7 0.0 copy-done.6
  302.7 0.6 copy.32
  303.3 0.0 copy-done
  303.3 1.2 copy.33
  304.5 0.0 copy-done.3
  304.5 0.8 copy.34
  305.4 0.0 copy-done.7
  305.4 0.6 copy.35
  305.9 0.0 copy-done.5
  305.9 0.6 copy.36
  306.5 0.0 copy-done.4
  306.5 0.6 copy.37
  (4 shorter events, 0.0 us)
Async XLA Ops:
  294.8 6.1 %copy-start.2 = (bf16[512,768]{1,0:T(8,128)(2,1)S(1)}, bf16[512,768]{1,0:T(8,128)(2,1)}, u32[]{:S(2)}) copy-start(bf16[512,768]{1,0:T(8,128)(2,1)} %get-tuple-element.90) | copy-start | bytes 2359300
  294.8 7.0 %copy-start.1 = (bf16[512,768]{1,0:T(8,128)(2,1)S(1)}, bf16[512,768]{1,0:T(8,128)(2,1)}, u32[]{:S(2)}) copy-start(bf16[512,768]{1,0:T(8,128)(2,1)} %get-tuple-element.91) | copy-start | bytes 2359300
  300.9 1.8 copy-start.6
  300.9 2.4 copy-start
  301.8 2.7 copy-start.3
  303.3 2.0 copy-start.7
  303.3 2.6 copy-start.5
  303.3 3.2 %copy-start.4 = (f32[8,768]{1,0:T(8,128)S(1)}, f32[8,768]{1,0:T(8,128)}, u32[]{:S(2)}) copy-start(f32[8,768]{1,0:T(8,128)} %get-tuple-element.74) | copy-start | bytes 73732

commit v3 on v2

--- a/solution.py
+++ b/solution.py
@@ -688,7 +688,7 @@
         pltpu.make_async_copy(normed_ref, block_ref.at[place], local_sem.at[1]),
     )
     each(own, lambda c: c.start())
-    rest = D // 4 * 3
+    rest = D // 8 * 5
     far_down = tensor_copy(down_ref.at[rest:], w_ref.at[1, D + rest :], y_send, y_recv, away)
     far_down.start()
     grads_load = pltpu.make_async_copy(grads_in, grads_ref, grads_sem)
@@ -1482,7 +1482,7 @@
         one.start()
     far = (
         tensor_copy(up_ref, far_up_ref, y_send.at[3], y_recv.at[3], away),
-        tensor_copy(down_ref.at[: D // 4 * 3], far_half_ref, y_send.at[4], y_recv.at[4], away),
+        tensor_copy(down_ref.at[: D // 8 * 5], far_half_ref, y_send.at[4], y_recv.at[4], away),
     )
 
     def along(block, step):
@@ -1606,7 +1606,7 @@
     ]
     outs = kept + [
         (half, F32), (half, BF), ((8, rows), F32), ((8, rows), F32), ((4 * local, D), BF), ((heads, NB), F32),
-        ((2, LINE, cap, D), BF), ((D, D), BF), ((D // 4 * 3, D), BF), ((2, rows, D), BF), ((2, 8, rows), F32),
+        ((2, LINE, cap, D), BF), ((D, D), BF), ((D // 8 * 5, D), BF), ((2, rows, D), BF), ((2, 8, rows), F32),
     ]
     shapes = [
         (half, BF), (half, BF), ((SEQ, D), F32), (half, F32), (half, BF), ((LINE, rows, D), BF), ((LINE, 8, rows), F32),

time: 314 us -> 312 us (level)
  the two profiles are of different devices: /device:TPU:14 before, /device:TPU:8 now
where the time goes in v3:
time: 312 us; the launch traced here: 306 us
  Pallas kernels  292 us (94%)
  local copies, waits for them, and re-layouts  6.19 us (2%)
  other arithmetic  6.09 us (2%)
    pallas_call x1, Pallas kernels, finish(): pl.pallas_call(functools.partial(finish_kernel, heads, cap), out_shape=[j...  109 us
    pallas_call x1, Pallas kernels, moe_line(): pl.pallas_call(functools.partial(expert_line_kernel, cap), out_shape=[jax...  105 us
    pallas_call x1, Pallas kernels, begin(): pl.pallas_call(functools.partial(begin_kernel, heads, cap), out_shape=[ja...  78.3 us

profile of v3, /device:TPU:8, one launch (start us, length us, event | category | flops | bytes accessed | tf_op | source)
XLA Modules:
  0.0 305.6 jit_solution(7353334135500492511)
XLA Ops:
  0.6 78.3 %begin.1 = (bf16[1024,768]{1,0:T(8,128)(2,1)}, bf16[576,1024]{1,0:T(8,128)(2,1)}, bf16[192,1024]{1,0:T(8,128)(2,1)}, f32[8,1024]{1,0:T(8,128)}, bf16[576,1024]{1...) custom-call(s32[2]{0:T(128)} %lengths_ref.3, ...), custom_call_target="tpu_custom_call" | custom-call | bytes 209715200 | tf_op jit(solution)/shard_map/begin/pallas_call | solution.py:1615
  79.0 104.9 %experts_line.1 = (bf16[2048,768]{1,0:T(8,128)(2,1)}, bf16[2048,768]{1,0:T(8,128)(2,1)}, bf16[1536,768]{1,0:T(8,128)(2,1)}, bf16[1536,768]{1,0:T(8,128)(2,1)}, b...) custom-call(bf16[512,768]{1,0:T(8,128)(2,1)} %get-tuple-element.46.normed_ref, f32[8,512]{1,0:T(8,128)} %get-tuple-element.47.info_in, ...), custom_call_target="tpu_custom_call" | custom-call | flops 57982058496 | bytes 62914560 | tf_op jit(solution)/shard_map/experts_line/pallas_call | solution.py:958
  183.9 108.9 %finish.1 = (bf16[512,768]{1,0:T(8,128)(2,1)}, bf16[512,768]{1,0:T(8,128)(2,1)}, f32[576,768]{1,0:T(8,128)}, f32[192,768]{1,0:T(8,128)}, f32[768]{0:T(1024)}, /*...) custom-call(s32[2]{0:T(128)} %lengths_ref.3, ...), custom_call_target="tpu_custom_call" | custom-call | bytes 209715200 | tf_op jit(solution)/shard_map/finish/pallas_call | solution.py:1384
  292.8 0.0 copy-start.2
  292.8 0.0 copy-start.1
  292.8 6.1 %add_bitcast_fusion = (f32[1,768,768]{2,1,0:T(8,128)}, f32[1,768,768]{2,1,0:T(8,128)}) fusion(bf16[1536,768]{1,0:T(8,128)(2,1)} %get-tuple-element.77, bf16[1536,768]{1,0:T(8,128)(2,1)} %get-tuple-element.76, bf16[1536,768]{1,0:T(8,128)(2,1)} %get-tuple-element.75), kind=kLoop, calls=%fused_computation | loop fusion | flops 5898240 | bytes 11796480 | tf_op jit(solution)/shard_map/broadcast_in_dim | solution.py:1845
  298.9 0.0 copy-start.6
  298.9 0.0 copy-start
  298.9 0.0 copy-done.2
  298.9 0.9 copy.30
  299.8 0.0 copy-done.1
  299.8 0.9 copy.31
  300.7 0.0 copy-done.6
  300.7 0.6 copy.32
  301.3 0.0 copy-done
  301.3 1.2 copy.33
  302.5 0.0 copy-done.3
  302.5 0.8 copy.34
  303.3 0.0 copy-done.7
  303.3 0.6 copy.35
  303.9 0.0 copy-done.5
  303.9 0.6 copy.36
  304.5 0.0 copy-done.4
  304.5 0.6 copy.37
  (4 shorter events, 0.0 us)
Async XLA Ops:
  292.8 6.1 %copy-start.2 = (bf16[512,768]{1,0:T(8,128)(2,1)S(1)}, bf16[512,768]{1,0:T(8,128)(2,1)}, u32[]{:S(2)}) copy-start(bf16[512,768]{1,0:T(8,128)(2,1)} %get-tuple-element.90) | copy-start | bytes 2359300
  292.8 7.0 %copy-start.1 = (bf16[512,768]{1,0:T(8,128)(2,1)S(1)}, bf16[512,768]{1,0:T(8,128)(2,1)}, u32[]{:S(2)}) copy-start(bf16[512,768]{1,0:T(8,128)(2,1)} %get-tuple-element.91) | copy-start | bytes 2359300
  298.9 1.8 copy-start.6
  298.9 2.4 copy-start
  299.8 2.7 copy-start.3
  301.3 2.0 copy-start.7
  301.3 2.6 copy-start.5
  301.3 3.2 %copy-start.4 = (f32[8,768]{1,0:T(8,128)S(1)}, f32[8,768]{1,0:T(8,128)}, u32[]{:S(2)}) copy-start(f32[8,768]{1,0:T(8,128)} %get-tuple-element.74) | copy-start | bytes 73732

commit v4 on v3

--- a/solution.py
+++ b/solution.py
@@ -688,7 +688,7 @@
         pltpu.make_async_copy(normed_ref, block_ref.at[place], local_sem.at[1]),
     )
     each(own, lambda c: c.start())
-    rest = D // 8 * 5
+    rest = D // 2
     far_down = tensor_copy(down_ref.at[rest:], w_ref.at[1, D + rest :], y_send, y_recv, away)
     far_down.start()
     grads_load = pltpu.make_async_copy(grads_in, grads_ref, grads_sem)
@@ -1482,7 +1482,7 @@
         one.start()
     far = (
         tensor_copy(up_ref, far_up_ref, y_send.at[3], y_recv.at[3], away),
-        tensor_copy(down_ref.at[: D // 8 * 5], far_half_ref, y_send.at[4], y_recv.at[4], away),
+        tensor_copy(down_ref.at[: D // 2], far_half_ref, y_send.at[4], y_recv.at[4], away),
     )
 
     def along(block, step):
@@ -1606,7 +1606,7 @@
     ]
     outs = kept + [
         (half, F32), (half, BF), ((8, rows), F32), ((8, rows), F32), ((4 * local, D), BF), ((heads, NB), F32),
-        ((2, LINE, cap, D), BF), ((D, D), BF), ((D // 8 * 5, D), BF), ((2, rows, D), BF), ((2, 8, rows), F32),
+        ((2, LINE, cap, D), BF), ((D, D), BF), ((D // 2, D), BF), ((2, rows, D), BF), ((2, 8, rows), F32),
     ]
     shapes = [
         (half, BF), (half, BF), ((SEQ, D), F32), (half, F32), (half, BF), ((LINE, rows, D), BF), ((LINE, 8, rows), F32),

time: 312 us -> 319 us (1.022)
  Pallas kernels: 292 us -> 300 us
    pallas_call x1, Pallas kernels: 109 us -> 114 us  [finish(): pl.pallas_call(functools.partial(finish_kernel, heads, cap), out_shape=[j...]
where the time goes in v4:
time: 319 us; the launch traced here: 313 us
  Pallas kernels  300 us (94%)
  local copies, waits for them, and re-layouts  6.19 us (2%)
  other arithmetic  6.09 us (2%)
    pallas_call x1, Pallas kernels, finish(): pl.pallas_call(functools.partial(finish_kernel, heads, cap), out_shape=[j...  114 us
    pallas_call x1, Pallas kernels, moe_line(): pl.pallas_call(functools.partial(expert_line_kernel, cap), out_shape=[jax...  108 us
    pallas_call x1, Pallas kernels, begin(): pl.pallas_call(functools.partial(begin_kernel, heads, cap), out_shape=[ja...  78.3 us

profile of v4, /device:TPU:8, one launch (start us, length us, event | category | flops | bytes accessed | tf_op | source)
XLA Modules:
  0.0 313.0 jit_solution(3127733327121263340)
XLA Ops:
  0.6 78.3 %begin.1 = (bf16[1024,768]{1,0:T(8,128)(2,1)}, bf16[576,1024]{1,0:T(8,128)(2,1)}, bf16[192,1024]{1,0:T(8,128)(2,1)}, f32[8,1024]{1,0:T(8,128)}, bf16[576,1024]{1...) custom-call(s32[2]{0:T(128)} %lengths_ref.3, ...), custom_call_target="tpu_custom_call" | custom-call | bytes 209715200 | tf_op jit(solution)/shard_map/begin/pallas_call | solution.py:1615
  79.0 107.7 %experts_line.1 = (bf16[2048,768]{1,0:T(8,128)(2,1)}, bf16[2048,768]{1,0:T(8,128)(2,1)}, bf16[1536,768]{1,0:T(8,128)(2,1)}, bf16[1536,768]{1,0:T(8,128)(2,1)}, b...) custom-call(bf16[512,768]{1,0:T(8,128)(2,1)} %get-tuple-element.46.normed_ref, f32[8,512]{1,0:T(8,128)} %get-tuple-element.47.info_in, ...), custom_call_target="tpu_custom_call" | custom-call | flops 57982058496 | bytes 62914560 | tf_op jit(solution)/shard_map/experts_line/pallas_call | solution.py:958
  186.7 113.6 %finish.1 = (bf16[512,768]{1,0:T(8,128)(2,1)}, bf16[512,768]{1,0:T(8,128)(2,1)}, f32[576,768]{1,0:T(8,128)}, f32[192,768]{1,0:T(8,128)}, f32[768]{0:T(1024)}, /*...) custom-call(s32[2]{0:T(128)} %lengths_ref.3, ...), custom_call_target="tpu_custom_call" | custom-call | bytes 209715200 | tf_op jit(solution)/shard_map/finish/pallas_call | solution.py:1384
  300.3 0.0 copy-start.2
  300.3 0.0 copy-start.1
  300.3 6.1 %add_bitcast_fusion = (f32[1,768,768]{2,1,0:T(8,128)}, f32[1,768,768]{2,1,0:T(8,128)}) fusion(bf16[1536,768]{1,0:T(8,128)(2,1)} %get-tuple-element.77, bf16[1536,768]{1,0:T(8,128)(2,1)} %get-tuple-element.76, bf16[1536,768]{1,0:T(8,128)(2,1)} %get-tuple-element.75), kind=kLoop, calls=%fused_computation | loop fusion | flops 5898240 | bytes 11796480 | tf_op jit(solution)/shard_map/broadcast_in_dim | solution.py:1845
  306.4 0.0 copy-start.6
  306.4 0.0 copy-start
  306.4 0.0 copy-done.2
  306.4 0.9 copy.30
  307.3 0.0 copy-done.1
  307.3 0.9 copy.31
  308.2 0.0 copy-done.6
  308.2 0.6 copy.32
  308.8 0.0 copy-done
  308.8 1.2 copy.33
  310.0 0.0 copy-done.3
  310.0 0.8 copy.34
  310.8 0.0 copy-done.7
  310.8 0.6 copy.35
  311.4 0.0 copy-done.5
  311.4 0.6 copy.36
  312.0 0.0 copy-done.4
  312.0 0.6 copy.37
  (4 shorter events, 0.0 us)
Async XLA Ops:
  300.3 6.1 %copy-start.2 = (bf16[512,768]{1,0:T(8,128)(2,1)S(1)}, bf16[512,768]{1,0:T(8,128)(2,1)}, u32[]{:S(2)}) copy-start(bf16[512,768]{1,0:T(8,128)(2,1)} %get-tuple-element.90) | copy-start | bytes 2359300
  300.3 7.0 %copy-start.1 = (bf16[512,768]{1,0:T(8,128)(2,1)S(1)}, bf16[512,768]{1,0:T(8,128)(2,1)}, u32[]{:S(2)}) copy-start(bf16[512,768]{1,0:T(8,128)(2,1)} %get-tuple-element.91) | copy-start | bytes 2359300
  306.4 1.8 copy-start.6
  306.4 2.4 copy-start
  307.3 2.7 copy-start.3
  308.8 2.0 copy-start.7
  308.8 2.6 copy-start.5
  308.8 3.2 %copy-start.4 = (f32[8,768]{1,0:T(8,128)S(1)}, f32[8,768]{1,0:T(8,128)}, u32[]{:S(2)}) copy-start(f32[8,768]{1,0:T(8,128)} %get-tuple-element.74) | copy-start | bytes 73732
